TPU v7x, 512 devices: a whole 4x8x8 slice. The times are simulated.
512 devices in a mesh: expert: 128 (over y, z, core), dp: 4 (over x).
Axes of the slice: x: 4, y: 8, z: 8, core: 2. Of those that a mesh axis runs over, the one named last changes fastest.
Arguments:
- tokens: bfloat16 [4096, 2048], P('expert', 'dp'), may hold values from -6 to 6
- out_grad: bfloat16 [4096, 2048], P('expert', 'dp'), may hold values from -6 to 6
- routes: int32 [4096, 8], P('expert'), may hold values from 0 to 127, all different within a row; in each aligned block of 32 rows (0 to 31, 32 to 63, ...) at most 2 rows name the same one
- route_weight: float32 [4096, 8], P('expert'), may hold values from 0.05 to 0.5
- placement: int32 [128], replicated, may hold values from 0 to 127, each once
- gate_weight: bfloat16 [128, 2048, 768], P('expert', 'dp'), may hold values from -0.125 to 0.125
- up_weight: bfloat16 [128, 2048, 768], P('expert', 'dp'), may hold values from -0.125 to 0.125
- down_weight: bfloat16 [128, 768, 2048], P('expert', None, 'dp'), may hold values from -0.21875 to 0.21875
Outputs:
- in_grad: bfloat16 [4096, 2048], P('expert', 'dp')
- gate_grad: bfloat16 [128, 2048, 768], P('expert', 'dp')
- up_grad: bfloat16 [128, 2048, 768], P('expert', 'dp')
- down_grad: bfloat16 [128, 768, 2048], P('expert', None, 'dp')
Inputs may be any that keep to these rules, and one draw needn't show every extreme that they name: `routes`: each row names 8 different experts. In each aligned block of 32 rows (the tokens of one index of the expert axis) no expert is named by more than 2 rows, a bound that some block reaches. `placement`: each index appears once.
All inputs are finite; a program needn't handle non-finite values.
Results may differ from a plain program's by a relative error of at most 0.025.
Values may be sent and summed in bfloat16 or wider, within the bound.
A program may use at most 64 MiB of HBM per device.

v0:
```python
import jax
import jax.numpy as jnp
from jax import lax
from jax.sharding import PartitionSpec as P


def product(left, right):
    return jnp.dot(left, right, preferred_element_type=jnp.float32)


def contract_cols(left, right):
    return lax.dot_general(
        left, right, (((1,), (1,)), ((), ())), preferred_element_type=jnp.float32
    )


def contract_rows(left, right):
    return lax.dot_general(
        left, right, (((0,), (0,)), ((), ())), preferred_element_type=jnp.float32
    )


def gate_backward(gate_sum, up_sum, hidden_grad):
    sigma = jax.nn.sigmoid(gate_sum)
    active = gate_sum * sigma
    hidden = (active * up_sum).astype(jnp.bfloat16)
    gate_back = (hidden_grad * up_sum * sigma * (1.0 + gate_sum * (1.0 - sigma))).astype(
        jnp.bfloat16
    )
    up_back = (hidden_grad * active).astype(jnp.bfloat16)
    return (hidden, gate_back, up_back)


def local(tokens, out_grad, routes, route_weight, placement, gate_weight, up_weight, down_weight):
    count_tok, width_part = tokens.shape
    chosen = routes.shape[1]
    hosts = lax.axis_size("expert")
    capacity = min(max(2, 7 * count_tok * chosen // (6 * hosts)), count_tok)
    total = hosts * capacity
    assigned = count_tok * chosen
    host_range = jnp.arange(hosts, dtype=jnp.int32)
    target = jnp.sum(
        jnp.where(routes[:, :, None] == host_range[None, None, :], placement[None, None, :], 0),
        axis=2,
    ).reshape(-1)
    onehot = (target[:, None] == host_range[None, :]).astype(jnp.int32)
    earlier = jnp.cumsum(onehot, axis=0) - onehot
    position = target * capacity + jnp.sum(earlier * onehot, axis=1)
    matched = position[None, :] == jnp.arange(total, dtype=jnp.int32)[:, None]
    filled = jnp.any(matched, axis=1)
    source = jnp.sum(jnp.where(matched, jnp.arange(assigned, dtype=jnp.int32)[None, :], 0), axis=1)
    token_row = source // chosen
    send_rows = jnp.where(
        filled[:, None], jnp.take(tokens, token_row, axis=0), jnp.zeros((), jnp.bfloat16)
    )
    weight_row = jnp.take(route_weight.reshape(-1), source)
    send_grad = jnp.where(
        filled[:, None],
        weight_row[:, None] * jnp.take(out_grad, token_row, axis=0).astype(jnp.float32),
        0.0,
    ).astype(jnp.bfloat16)
    moved_rows, moved_grad = (
        lax.all_to_all(
            send_rows.reshape(hosts, capacity, width_part),
            "expert",
            split_axis=0,
            concat_axis=0,
            tiled=True,
        ),
        lax.all_to_all(
            send_grad.reshape(hosts, capacity, width_part),
            "expert",
            split_axis=0,
            concat_axis=0,
            tiled=True,
        ),
    )
    rows_in = moved_rows.reshape(total, width_part)
    grad_in = moved_grad.reshape(total, width_part)
    gate_part = gate_weight[0]
    up_part = up_weight[0]
    down_part = down_weight[0]
    gate_sum, up_sum, hidden_grad = (
        lax.psum(product(rows_in, gate_part).astype(jnp.bfloat16), "dp").astype(jnp.float32),
        lax.psum(product(rows_in, up_part).astype(jnp.bfloat16), "dp").astype(jnp.float32),
        lax.psum(contract_cols(grad_in, down_part).astype(jnp.bfloat16), "dp").astype(jnp.float32),
    )
    hidden, gate_back, up_back = gate_backward(gate_sum, up_sum, hidden_grad)
    input_back = (contract_cols(gate_back, gate_part) + contract_cols(up_back, up_part)).astype(
        jnp.bfloat16
    )
    returned = lax.all_to_all(
        input_back.reshape(hosts, capacity, width_part),
        "expert",
        split_axis=0,
        concat_axis=0,
        tiled=True,
    ).reshape(total, width_part)
    in_grad = jnp.sum(
        jnp.take(returned, position, axis=0)
        .reshape(count_tok, chosen, width_part)
        .astype(jnp.float32),
        axis=1,
    ).astype(jnp.bfloat16)
    gate_grad = contract_rows(rows_in, gate_back).astype(jnp.bfloat16)[None]
    up_grad = contract_rows(rows_in, up_back).astype(jnp.bfloat16)[None]
    down_grad = contract_rows(hidden, grad_in).astype(jnp.bfloat16)[None]
    return (in_grad, gate_grad, up_grad, down_grad)


def solution(mesh):
    in_specs = (
        P("expert", "dp"),
        P("expert", "dp"),
        P("expert", None),
        P("expert", None),
        P(),
        P("expert", "dp", None),
        P("expert", "dp", None),
        P("expert", None, "dp"),
    )
    out_specs = (
        P("expert", "dp"),
        P("expert", "dp", None),
        P("expert", "dp", None),
        P("expert", None, "dp"),
    )
    return jax.shard_map(local, mesh=mesh, in_specs=in_specs, out_specs=out_specs, check_vma=False)
```

profile of v0, /device:TPU:1, one launch (start us, length us, event | category | flops | bytes accessed | tf_op | source)
XLA Modules:
  0.0 160.0 jit_solution(17797994856089147649)
XLA Ops:
  7.2 0.8 copy.17
  8.0 1.3 select_reduce_fusion.1
  9.7 0.2 fusion.22
  10.0 0.2 fusion.24
  10.2 0.1 fusion.21
  10.5 1.2 gather_fusion.3
  11.6 0.1 select_select_fusion
  11.8 0.8 reshape.138
  12.6 18.4 %all-to-all-start.1 = ((bf16[128,2,512]{2,1,0:T(2,128)(2,1)}), bf16[128,2,512]{2,1,0:T(2,128)(2,1)S(1)}, u32[]{:S(2)}, u32[]{:S(2)}) async-start(bf16[128,2,512]{2,1,0:T(2,128)(2,1)} %reshape.138), calls=%async_computation.1 | async-start | bytes 524288 | tf_op jit(solution)/shard_map/all_to_all | solution.py:63
  31.2 1.2 gather_fusion.2
  32.4 1.9 %gather_fusion = f32[256]{0:T(256)S(1)} fusion(f32[256]{0:T(256)S(1)} %reshape.135, s32[1024]{0:T(1024)S(1)} %pad_clamp_fusion.2), kind=kCustom, calls=%fused_computation.2 | custom fusion | bytes 3072 | tf_op jit(solution)/shard_map/jit(_take)/gather | solution.py:56
  34.3 0.2 select_convert_fusion
  34.5 0.8 reshape.136
  35.3 9.9 %all-to-all-done.1 = bf16[128,2,512]{2,1,0:T(2,128)(2,1)S(1)} async-done(((bf16[128,2,512]{2,1,0:T(2,128)(2,1)}), bf16[128,2,512]{2,1,0:T(2,128)(2,1)S(1)}, u32[]{:S(2)}, u32[]{:S(2)}) %all-to-all-start.1) | async-done | bytes 262176 | tf_op jit(solution)/shard_map/all_to_all | solution.py:63
  45.2 7.0 %all-to-all-start = ((bf16[128,2,512]{2,1,0:T(2,128)(2,1)}), bf16[128,2,512]{2,1,0:T(2,128)(2,1)S(1)}, u32[]{:S(2)}, u32[]{:S(2)}) async-start(bf16[128,2,512]{2,1,0:T(2,128)(2,1)} %reshape.136), calls=%async_computation | async-start | bytes 524288 | tf_op jit(solution)/shard_map/all_to_all | solution.py:70
  52.4 1.1 convolution_convert_fusion.3
  53.5 1.1 convolution_convert_fusion.4
  54.6 11.9 %all-to-all-done = bf16[128,2,512]{2,1,0:T(2,128)(2,1)S(1)} async-done(((bf16[128,2,512]{2,1,0:T(2,128)(2,1)}), bf16[128,2,512]{2,1,0:T(2,128)(2,1)S(1)}, u32[]{:S(2)}, u32[]{:S(2)}) %all-to-all-start) | async-done | bytes 262176 | tf_op jit(solution)/shard_map/all_to_all | solution.py:70
  66.7 1.1 convolution_convert_fusion.5
  68.1 49.3 %all-reduce.3.cloned.1.call-done = (bf16[256,768]{1,0:T(8,128)(2,1)}, bf16[256,768]{1,0:T(8,128)(2,1)}, bf16[256,768]{1,0:T(8,128)(2,1)}) async-done(((bf16[256,768]{1,0:T(8,128)(2,1)}, bf16[256,768]{1,0:T(8,128)(2,1)}, bf16[256,768]{1,0:T(8,128)(2,1)}), (bf16[256,768]{1,0:T(8,128)(2,1)}, bf16[256,768]{1,0:T(8,128)(2,1)}, bf16[256,768]{1,0:T(8,128)(2,1)})) %all-reduce.3.cloned.1.call-update) | async-done | bytes 1179664 | tf_op jit(solution)/shard_map/psum | solution.py:85
  117.4 1.6 fusion.7
  119.0 0.4 fusion.13
  119.4 0.6 copy-done.6
  120.1 0.4 fusion.3
  120.5 0.8 reshape.140
  121.3 15.5 %all-to-all-start.2 = ((bf16[128,2,512]{2,1,0:T(2,128)(2,1)}), bf16[128,2,512]{2,1,0:T(2,128)(2,1)S(1)}, u32[]{:S(2)}, u32[]{:S(2)}) async-start(bf16[128,2,512]{2,1,0:T(2,128)(2,1)} %reshape.140), calls=%async_computation.2 | async-start | bytes 524288 | tf_op jit(solution)/shard_map/all_to_all | solution.py:92
  136.9 1.3 fusion
  138.2 1.4 fusion.1
  139.6 1.3 fusion.2
  140.9 10.1 %all-to-all-done.2 = bf16[128,2,512]{2,1,0:T(2,128)(2,1)S(1)} async-done(((bf16[128,2,512]{2,1,0:T(2,128)(2,1)}), bf16[128,2,512]{2,1,0:T(2,128)(2,1)S(1)}, u32[]{:S(2)}, u32[]{:S(2)}) %all-to-all-start.2) | async-done | bytes 262176 | tf_op jit(solution)/shard_map/all_to_all | solution.py:92
  151.2 1.2 gather_fusion.1
  152.3 0.8 fusion.20
  (50 shorter events, 1.4 us)
Async XLA Ops:
  7.2 45.2 %copy-start = (bf16[1,512,768]{2,1,0:T(8,128)(2,1)S(1)}, bf16[1,512,768]{2,1,0:T(8,128)(2,1)}, u32[]{:S(2)}) copy-start(bf16[1,512,768]{2,1,0:T(8,128)(2,1)} %param.15) | copy-start | bytes 2359300
  7.2 3.3 %copy-start.1 = (bf16[32,512]{1,0:T(8,128)(2,1)S(1)}, bf16[32,512]{1,0:T(8,128)(2,1)}, u32[]{:S(2)}) copy-start(bf16[32,512]{1,0:T(8,128)(2,1)} %param.10) | copy-start | bytes 98308
  11.6 19.4 %copy-start.10 = (f32[32,8]{0,1:T(8,128)S(1)}, f32[32,8]{0,1:T(8,128)}, u32[]{:S(2)}) copy-start(f32[32,8]{0,1:T(8,128)} %param.13) | copy-start | bytes 3076
  11.6 19.6 %copy-start.2 = (bf16[32,512]{1,0:T(8,128)(2,1)S(1)}, bf16[32,512]{1,0:T(8,128)(2,1)}, u32[]{:S(2)}) copy-start(bf16[32,512]{1,0:T(8,128)(2,1)} %param.11) | copy-start | bytes 98308
  12.6 32.7 %all-to-all-start.1 = ((bf16[128,2,512]{2,1,0:T(2,128)(2,1)}), bf16[128,2,512]{2,1,0:T(2,128)(2,1)S(1)}, u32[]{:S(2)}, u32[]{:S(2)}) async-start(bf16[128,2,512]{2,1,0:T(2,128)(2,1)} %reshape.138), calls=%async_computation.1 | async-start | bytes 524288 | tf_op jit(solution)/shard_map/all_to_all | solution.py:63
  45.2 21.3 %all-to-all-start = ((bf16[128,2,512]{2,1,0:T(2,128)(2,1)}), bf16[128,2,512]{2,1,0:T(2,128)(2,1)S(1)}, u32[]{:S(2)}, u32[]{:S(2)}) async-start(bf16[128,2,512]{2,1,0:T(2,128)(2,1)} %reshape.136), calls=%async_computation | async-start | bytes 524288 | tf_op jit(solution)/shard_map/all_to_all | solution.py:70
  52.2 65.2 %all-reduce.3.cloned.1.call-start = ((), (), s32[]{:S(2)}) async-start(), calls=%async_computation.3 | async-start | bytes 2359296 | tf_op jit(solution)/shard_map/psum | solution.py:85
  52.4 1.1 copy-start.4
  53.5 13.2 %copy-start.3 = (bf16[1,768,512]{2,1,0:T(8,128)(2,1)S(1)}, bf16[1,768,512]{2,1,0:T(8,128)(2,1)}, u32[]{:S(2)}) copy-start(bf16[1,768,512]{2,1,0:T(8,128)(2,1)} %param.17) | copy-start | bytes 2359300
  119.0 1.0 copy-start.6
  119.0 1.1 copy-start.8
  121.3 29.8 %all-to-all-start.2 = ((bf16[128,2,512]{2,1,0:T(2,128)(2,1)}), bf16[128,2,512]{2,1,0:T(2,128)(2,1)S(1)}, u32[]{:S(2)}, u32[]{:S(2)}) async-start(bf16[128,2,512]{2,1,0:T(2,128)(2,1)} %reshape.140), calls=%async_computation.2 | async-start | bytes 524288 | tf_op jit(solution)/shard_map/all_to_all | solution.py:92
  136.8 1.3 copy-start.7
  136.9 1.3 copy-start.9
  138.2 1.4 copy-start.5
Sparse Core Ops, SparseCore 0:
  68.0 49.3 all-reduce.2
where the time goes:
time: 160 us
  waiting for transfers between devices  81.3 us (51%)
  starting transfers between devices  41 us (26%)
  between operations  14.3 us (9%)
  local copies, waits for them, and re-layouts  10.4 us (6%)
  matrix products  8.25 us (5%)
  other arithmetic  4.79 us (3%)
    psum x1, waiting for transfers between devices, local(): lax.psum(product(rows_in, up_part).astype(jnp.bfloat16), 'dp')  49.3 us
    all_to_all x1, starting transfers between devices, local(): lax.all_to_all(send_rows.reshape(hosts, capacity, width_part), 'expert',...  18.4 us
    all_to_all x1, starting transfers between devices, local(): lax.all_to_all(input_back.reshape(hosts, capacity, width_part), 'expert',...  15.5 us
    all_to_all x1, waiting for transfers between devices, local(): lax.all_to_all(send_grad.reshape(hosts, capacity, width_part), 'expert',...  11.9 us
    all_to_all x1, waiting for transfers between devices, local(): lax.all_to_all(input_back.reshape(hosts, capacity, width_part), 'expert',...  10.1 us
    all_to_all x1, waiting for transfers between devices, local(): lax.all_to_all(send_rows.reshape(hosts, capacity, width_part), 'expert',...  9.91 us
    all_to_all x1, starting transfers between devices, local(): lax.all_to_all(send_grad.reshape(hosts, capacity, width_part), 'expert',...  6.96 us
    dot_general x3, matrix products, contract_rows(): lax.dot_general(left, right, (((0,), (0,)), ((), ())), preferred_element_...  4.06 us
  transfers between devices with their start and end apart: 4, of which 4 were waited for; matrix products, arithmetic and copies ran while one was open for 7% of the time, Pallas kernels for 0%

commit v1 on v0

v1 whole, which is shorter than its diff:
```python
import functools

import jax
import jax.numpy as jnp
from jax import lax
from jax.experimental import pallas as pl
from jax.experimental.pallas import tpu as pltpu
from jax.sharding import PartitionSpec as P

BF = jnp.bfloat16
F32 = jnp.float32
LANES = 128


def matmul(left, right, left_dim=1, right_dim=0):
    return lax.dot_general(
        left, right, (((left_dim,), (right_dim,)), ((), ())), preferred_element_type=F32
    )


def remote(src, dst, send_sem, recv_sem, device):
    return pltpu.make_async_remote_copy(
        src_ref=src,
        dst_ref=dst,
        send_sem=send_sem,
        recv_sem=recv_sem,
        device_id=device,
        device_id_type=pl.DeviceIdType.MESH,
    )


def kernel(
    side, parts,
    tokens, out_grad, routes, route_weight, placement, gate_hbm, up_hbm, down_hbm,
    in_grad, gate_grad_hbm, up_grad_hbm, down_grad_hbm,
    gate, up, down, gate_grad, up_grad, down_grad,
    send0, send1, mid0, mid1, recv, rows_all, grad_all,
    psend, precv, full, ret, rmid, fin0, fin1, spread, select,
    load_sem, store_sem, s1_send, s1_recv, s2_send, s2_recv,
    p_send, p_recv, a_send, a_recv, r1_send, r1_recv, r2_send, r2_recv,
):
    n = side
    experts = 2 * n * n
    count_tok, width = tokens.shape
    chunks = width // LANES
    units = 2 * chunks
    hidden_dim = gate.shape[1]
    chosen = routes.shape[1]
    span = experts // parts
    me = lax.axis_index("expert")
    d = lax.axis_index("dp")
    y = me // (2 * n)
    z = lax.rem(me // 2, n)
    c = lax.rem(me, 2)

    def at(yy, zz, cc):
        return {"expert": (yy * n + zz) * 2 + cc}

    def turn(base, i):
        return lax.rem(base + i, n)

    loads = [
        pltpu.make_async_copy(src.at[0], dst, load_sem.at[i])
        for i, (src, dst) in enumerate(((gate_hbm, gate), (up_hbm, up), (down_hbm, down)))
    ]
    for load in loads:
        load.start()

    barrier = pltpu.get_barrier_semaphore()
    greeted = [at(y, z, 1 - c)]
    for i in range(1, n):
        for cc in range(2):
            greeted += [at(turn(y, i), z, cc), at(y, turn(z, i), cc)]
    greeted += [{"dp": lax.rem(d + i, parts)} for i in range(1, parts)]
    for device in greeted:
        pl.semaphore_signal(
            barrier, inc=1, device_id=device, device_id_type=pl.DeviceIdType.MESH
        )

    place = placement[...]
    place_y, place_z, place_c = place // (2 * n), lax.rem(place // 2, n), lax.rem(place, 2)
    spot = jnp.where(place_c == 0, place_y * n + place_z, n * n + place_z * n + place_y)
    spot = spot.astype(F32)
    expert_ids = lax.broadcasted_iota(jnp.int32, (count_tok, experts), 1)
    expert_ids_f = expert_ids.astype(F32)
    named = jnp.zeros((count_tok, experts), F32)
    weight = jnp.zeros((count_tok, experts), F32)
    for k in range(chosen):
        hit = routes[:, k : k + 1] == expert_ids
        where = jnp.sum(jnp.where(hit, spot, 0.0), axis=1, keepdims=True)
        mine = where == expert_ids_f
        named = jnp.where(mine, 1.0, named)
        weight = jnp.where(mine, route_weight[:, k : k + 1], weight)
    before = (
        lax.broadcasted_iota(jnp.int32, (count_tok, count_tok), 0)
        > lax.broadcasted_iota(jnp.int32, (count_tok, count_tok), 1)
    ).astype(BF)
    rank = matmul(before, named.astype(BF))

    for r in range(2):
        chosen_rank = rank < 0.5 if r == 0 else rank > 0.5
        pick = jnp.where(chosen_rank, named, 0.0)
        select[r] = pick.astype(BF)
        row_weight = jnp.sum(pick * weight, axis=0, keepdims=True)
        row_weight = jnp.transpose(jnp.broadcast_to(row_weight, (LANES, experts)))
        token_rows = matmul(select[r], tokens[...], 0, 0)
        grad_rows = matmul(select[r], out_grad[...], 0, 0)
        for j in range(chunks):
            lanes = slice(j * LANES, (j + 1) * LANES)
            spread[r, pl.ds(j, experts, stride=units), :] = token_rows[:, lanes]
            spread[r, pl.ds(chunks + j, experts, stride=units), :] = (
                row_weight * grad_rows[:, lanes]
            )
        ready = spread[r].astype(BF).reshape(2, n, n, units, LANES)
        send0[r] = ready[0]
        send1[r] = ready[1]

    pl.semaphore_wait(barrier, len(greeted))

    for r in range(2):
        for i in range(1, n):
            yy, zz = turn(y, i), turn(z, i)
            remote(
                send0.at[r, yy], mid0.at[r, y], s1_send.at[r, 0], s1_recv.at[r, 0], at(yy, z, c)
            ).start()
            remote(
                send1.at[r, zz], mid1.at[r, z], s1_send.at[r, 1], s1_recv.at[r, 1], at(y, zz, c)
            ).start()
        mid0[r, y] = send0[r, y]
        mid1[r, z] = send1[r, z]

    some = at(y, z, 1 - c)
    for r in range(2):
        for p, (sent, mid) in enumerate(((send0, mid0), (send1, mid1))):
            if n > 1:
                part = pl.ds(0, n - 1)
                remote(
                    sent.at[r, part], mid.at[r, part], s1_send.at[r, p], s1_recv.at[r, p], some
                ).wait()
            base, slot = ((z, z * 2 + c), (y, y * 2 + c))[p]
            for i in range(1, n):
                other = turn(base, i)
                device = at(y, other, 0) if p == 0 else at(other, z, 1)
                remote(
                    mid.at[r, :, other], recv.at[r, slot], s2_send.at[r], s2_recv.at[r], device
                ).start()

            @pl.when(c == p)
            def _():
                recv[r, slot] = mid[r, :, base]

            @pl.when(c != p)
            def _():
                remote(
                    mid.at[r, :, base], recv.at[r, slot], s2_send.at[r], s2_recv.at[r], some
                ).start()

    for r in range(2):
        part = pl.ds(0, 2 * n - 1)
        remote(recv.at[r, part], recv.at[r, part], s2_send.at[r], s2_recv.at[r], some).wait()
        spread[r] = recv[r].reshape(experts * units, LANES).astype(F32)
        rows = slice(r * experts, (r + 1) * experts)
        for j in range(chunks):
            lanes = slice(j * LANES, (j + 1) * LANES)
            rows_all[rows, lanes] = spread[r, pl.ds(j, experts, stride=units), :].astype(BF)
            grad_all[rows, lanes] = spread[r, pl.ds(chunks + j, experts, stride=units), :].astype(BF)
        if r == 0:
            for load in loads:
                load.wait()
        shape = (parts, span, hidden_dim)
        psend[r, :, :, 0:hidden_dim] = (
            matmul(rows_all[rows, :], gate[...]).astype(BF).reshape(shape)
        )
        psend[r, :, :, hidden_dim : 2 * hidden_dim] = (
            matmul(rows_all[rows, :], up[...]).astype(BF).reshape(shape)
        )
        psend[r, :, :, 2 * hidden_dim :] = (
            matmul(grad_all[rows, :], down[...], 1, 1).astype(BF).reshape(shape)
        )
        for i in range(1, parts):
            q = lax.rem(d + i, parts)
            remote(
                psend.at[r, q], precv.at[r, i - 1], p_send.at[r, i - 1], p_recv.at[r, i - 1],
                {"dp": q},
            ).start()

    for r in range(2):
        total = psend[r, d].astype(F32)
        for i in range(1, parts):
            remote(
                psend.at[r, i], precv.at[r, i - 1], p_send.at[r, i - 1], p_recv.at[r, i - 1],
                {"dp": lax.rem(d + i, parts)},
            ).wait()
            total = total + precv[r, i - 1].astype(F32)
        gate_sum = total[:, 0:hidden_dim]
        up_sum = total[:, hidden_dim : 2 * hidden_dim]
        hidden_grad = total[:, 2 * hidden_dim :]
        sigma = jax.nn.sigmoid(gate_sum)
        active = gate_sum * sigma
        full[r, d, :, 0:hidden_dim] = (active * up_sum).astype(BF)
        full[r, d, :, hidden_dim : 2 * hidden_dim] = (
            hidden_grad * up_sum * sigma * (1.0 + gate_sum * (1.0 - sigma))
        ).astype(BF)
        full[r, d, :, 2 * hidden_dim :] = (hidden_grad * active).astype(BF)
        for i in range(1, parts):
            remote(
                full.at[r, d], full.at[r, d], a_send.at[r, i - 1], a_recv.at[r, i - 1],
                {"dp": lax.rem(d + i, parts)},
            ).start()

    for r in range(2):
        for i in range(1, parts):
            q = lax.rem(d + parts - i, parts)
            remote(
                full.at[r, q], full.at[r, q], a_send.at[r, i - 1], a_recv.at[r, i - 1], {"dp": q}
            ).wait()
        gate_back = full[r, :, :, hidden_dim : 2 * hidden_dim].reshape(experts, hidden_dim)
        up_back = full[r, :, :, 2 * hidden_dim :].reshape(experts, hidden_dim)
        row_back = matmul(gate_back, gate[...], 1, 1) + matmul(up_back, up[...], 1, 1)
        for j in range(chunks):
            spread[0, pl.ds(r * chunks + j, experts, stride=units), :] = row_back[
                :, j * LANES : (j + 1) * LANES
            ]
    ret[...] = spread[0].astype(BF).reshape(2 * n, n, units, LANES)

    base = jnp.where(c == 0, z, y)
    own = base * 2 + c
    back = c * n + base
    for i in range(1, 2 * n):
        j = lax.rem(own + i, 2 * n)
        jj, jc = j // 2, lax.rem(j, 2)
        device = at(jnp.where(c == 0, y, jj), jnp.where(c == 0, jj, z), jc)
        remote(ret.at[j], rmid.at[back], r1_send, r1_recv, device).start()
    rmid[back] = ret[own]

    stores = []
    for i, (left, first, result, out) in enumerate(
        ((rows_all, 1, gate_grad, gate_grad_hbm), (rows_all, 2, up_grad, up_grad_hbm))
    ):
        right = full[:, :, :, first * hidden_dim : (first + 1) * hidden_dim]
        result[...] = matmul(left[...], right.reshape(2 * experts, hidden_dim), 0, 0).astype(BF)
        stores.append(pltpu.make_async_copy(result, out.at[0], store_sem.at[i]))
        stores[-1].start()
    hidden = full[:, :, :, 0:hidden_dim].reshape(2 * experts, hidden_dim)
    down_grad[...] = matmul(hidden, grad_all[...], 0, 0).astype(BF)
    stores.append(pltpu.make_async_copy(down_grad, down_grad_hbm.at[0], store_sem.at[2]))
    stores[-1].start()

    part = pl.ds(0, 2 * n - 1)
    remote(ret.at[part], rmid.at[part], r1_send, r1_recv, some).wait()
    for i in range(1, n):
        yy, zz = turn(y, i), turn(z, i)
        remote(
            rmid.at[pl.ds(0, n), yy], fin0.at[y], r2_send.at[0], r2_recv.at[0], at(yy, z, c)
        ).start()
        remote(
            rmid.at[pl.ds(n, n), zz], fin1.at[z], r2_send.at[1], r2_recv.at[1], at(y, zz, c)
        ).start()
    fin0[y] = rmid[0:n, y]
    fin1[z] = rmid[n : 2 * n, z]
    if n > 1:
        part = pl.ds(0, n - 1)
        for p, fin in enumerate((fin0, fin1)):
            remote(fin.at[part], fin.at[part], r2_send.at[p], r2_recv.at[p], some).wait()

    half = n * n * units
    spread[1, 0:half, :] = fin0[...].reshape(half, LANES).astype(F32)
    spread[1, half : 2 * half, :] = fin1[...].reshape(half, LANES).astype(F32)
    for j in range(chunks):
        total = jnp.zeros((count_tok, LANES), F32)
        for r in range(2):
            came = spread[1, pl.ds(r * chunks + j, experts, stride=units), :].astype(BF)
            total = total + matmul(select[r], came)
        in_grad[:, j * LANES : (j + 1) * LANES] = total.astype(BF)
    for store in stores:
        store.wait()


def local(tokens, out_grad, routes, route_weight, placement, gate_weight, up_weight, down_weight):
    experts = lax.axis_size("expert")
    parts = lax.axis_size("dp")
    side = 1
    while 2 * side * side < experts:
        side *= 2
    n = side
    count_tok, width = tokens.shape
    _, _, hidden_dim = gate_weight.shape
    units = 2 * width // LANES
    span = experts // parts
    vmem = pl.BlockSpec(memory_space=pltpu.VMEM)
    hbm = pl.BlockSpec(memory_space=pl.ANY)
    dma = pltpu.SemaphoreType.DMA

    def buf(*shape, dtype=BF):
        return pltpu.VMEM(shape, dtype)

    return pl.pallas_call(
        functools.partial(kernel, side, parts),
        out_shape=(
            jax.ShapeDtypeStruct((count_tok, width), BF),
            jax.ShapeDtypeStruct(gate_weight.shape, BF),
            jax.ShapeDtypeStruct(up_weight.shape, BF),
            jax.ShapeDtypeStruct(down_weight.shape, BF),
        ),
        in_specs=[vmem] * 5 + [hbm] * 3,
        out_specs=(vmem, hbm, hbm, hbm),
        scratch_shapes=[
            buf(width, hidden_dim), buf(width, hidden_dim), buf(hidden_dim, width),
            buf(width, hidden_dim), buf(width, hidden_dim), buf(hidden_dim, width),
            buf(2, n, n, units, LANES), buf(2, n, n, units, LANES),
            buf(2, n, n, units, LANES), buf(2, n, n, units, LANES),
            buf(2, 2 * n, n, units, LANES),
            buf(2 * experts, width), buf(2 * experts, width),
            buf(2, parts, span, 3 * hidden_dim),
            buf(2, parts - 1, span, 3 * hidden_dim),
            buf(2, parts, span, 3 * hidden_dim),
            buf(2 * n, n, units, LANES), buf(2 * n, n, units, LANES),
            buf(n, n, units, LANES), buf(n, n, units, LANES),
            buf(2, experts * units, LANES, dtype=F32),
            buf(2, count_tok, experts),
            dma((3,)), dma((3,)),
            dma((2, 2)), dma((2, 2)), dma((2,)), dma((2,)),
            dma((2, parts - 1)), dma((2, parts - 1)), dma((2, parts - 1)), dma((2, parts - 1)),
            dma, dma, dma((2,)), dma((2,)),
        ],
        compiler_params=pltpu.CompilerParams(
            collective_id=0, has_side_effects=True, vmem_limit_bytes=48 << 20
        ),
        name="expert_backward",
    )(
        tokens, out_grad, routes, route_weight, placement.reshape(1, experts),
        gate_weight, up_weight, down_weight,
    )


def solution(mesh):
    in_specs = (
        P("expert", "dp"),
        P("expert", "dp"),
        P("expert", None),
        P("expert", None),
        P(),
        P("expert", "dp", None),
        P("expert", "dp", None),
        P("expert", None, "dp"),
    )
    out_specs = (
        P("expert", "dp"),
        P("expert", "dp", None),
        P("expert", "dp", None),
        P("expert", None, "dp"),
    )
    return jax.shard_map(local, mesh=mesh, in_specs=in_specs, out_specs=out_specs, check_vma=False)
```

time: 160 us -> 80.8 us (0.51)
  waiting for transfers between devices: 81.3 us -> 0 us
  Pallas kernels: 0 us -> 70.4 us
  starting transfers between devices: 41 us -> 0 us
  between operations: 14.3 us -> 0.66 us
  matrix products: 8.25 us -> 0 us
  other arithmetic: 4.79 us -> 0 us
    pallas_call x0 -> x1, Pallas kernels: none -> 70.4 us  [local(): pl.pallas_call(functools.partial(kernel, side, parts), out_shape=(jax.Sha...]
    psum x1 -> x0, waiting for transfers between devices: 49.3 us -> none  [local(): lax.psum(product(rows_in, up_part).astype(jnp.bfloat16), 'dp')]
    all_to_all x3 -> x0, starting transfers between devices: 40.9 us -> none  [the longest x1 18.4 us: local(): lax.all_to_all(send_rows.reshape(hosts, capacity, width_part), 'expert',...]
    all_to_all x3 -> x0, waiting for transfers between devices: 32 us -> none  [the longest x1 11.9 us: local(): lax.all_to_all(send_grad.reshape(hosts, capacity, width_part), 'expert',...]
    dot_general x8 -> x0, matrix products: 8.25 us -> none  [the longest x3 4.06 us: contract_rows(): lax.dot_general(left, right, (((0,), (0,)), ((), ())), preferred_element_...]
    unnamed x25 -> x18, local copies, waits for them, and re-layouts: 1.67 us -> 8.96 us
    gather x4 -> x0, local copies, waits for them, and re-layouts: 5.4 us -> none  [the longest x1 1.94 us: local(): weight_row = jnp.take(route_weight.reshape(-1), source)]
    reshape x8 -> x0, local copies, waits for them, and re-layouts: 2.9 us -> none  [the longest x1 0.8 us: local(): send_rows.reshape(hosts, capacity, width_part)]
  transfers between devices with their start and end apart: 4 -> 0, of which waited for: 4 -> 0; matrix products, arithmetic and copies ran while one was open for 7% -> 0% of each run, Pallas kernels for 0% -> 0%
where the time goes in v1:
time: 80.8 us; the launch traced here: 80 us
  Pallas kernels  70.4 us (87%)
  local copies, waits for them, and re-layouts  8.96 us (11%)
    pallas_call x1, Pallas kernels, local(): pl.pallas_call(functools.partial(kernel, side, parts), out_shape=(jax.Sha...  70.4 us
    unnamed x18, local copies, waits for them, and re-layouts  8.96 us

profile of v1, /device:TPU:1, one launch (start us, length us, event | category | flops | bytes accessed | tf_op | source)
XLA Modules:
  0.0 80.0 jit_solution(18205336880554690020)
XLA Ops:
  0.6 0.0 copy-start.3
  0.6 0.8 copy.12.routes
  1.4 0.0 copy-start.5
  1.4 0.8 copy.13.route_weight
  2.2 0.0 copy-done.3
  2.2 0.0 copy-done.5
  2.2 0.0 copy-start
  2.2 1.1 %copy-done = bf16[1,512,768]{2,1,0:T(8,128)(2,1)S(1)} copy-done((bf16[1,512,768]{2,1,0:T(8,128)(2,1)S(1)}, bf16[1,512,768]{2,1,0:T(8,128)(2,1)}, u32[]{:S(2)}) %copy-start) | copy-done | bytes 786456
  3.3 0.0 copy-start.1
  3.3 1.1 %copy-done.1 = bf16[1,512,768]{2,1,0:T(8,128)(2,1)S(1)} copy-done((bf16[1,512,768]{2,1,0:T(8,128)(2,1)S(1)}, bf16[1,512,768]{2,1,0:T(8,128)(2,1)}, u32[]{:S(2)}) %copy-start.1) | copy-done | bytes 786456
  4.5 0.0 copy-start.2
  4.5 1.1 %copy-done.2 = bf16[1,768,512]{2,1,0:T(8,128)(2,1)S(1)} copy-done((bf16[1,768,512]{2,1,0:T(8,128)(2,1)S(1)}, bf16[1,768,512]{2,1,0:T(8,128)(2,1)}, u32[]{:S(2)}) %copy-start.2) | copy-done | bytes 786456
  5.6 0.0 copy-start.4
  5.6 0.8 copy-done.4
  6.4 70.4 %expert_backward.1 = (bf16[32,512]{1,0:T(8,128)(2,1)S(1)}, bf16[1,512,768]{2,1,0:T(8,128)(2,1)S(1)}, bf16[1,512,768]{2,1,0:T(8,128)(2,1)S(1)}, bf16[1,768,512]{2,1,0:T(8,128)(2,1)S(1)}) custom-call(bf16[32,512]{1,0:T(8,128)(2,1)S(1)} %copy-done.3, bf16[32,512]{1,0:T(8,128)(2,1)S(1)} %copy-done.4, s32[32,8]{1,0:T(8,128)S(1)} %copy.12.routes, ...), custom_call_target="tpu_custom_call" | custom-call | tf_op jit(solution)/shard_map/expert_backward/pallas_call | solution.py:297
  76.7 0.6 copy.18
  77.4 0.9 %copy.19 = bf16[1,512,768]{2,1,0:T(8,128)(2,1)} copy(bf16[1,512,768]{2,1,0:T(8,128)(2,1)S(1)} %get-tuple-element.9) | data formatting | bytes 1572864
  78.2 0.9 %copy.20 = bf16[1,512,768]{2,1,0:T(8,128)(2,1)} copy(bf16[1,512,768]{2,1,0:T(8,128)(2,1)S(1)} %get-tuple-element.10) | data formatting | bytes 1572864
  79.1 0.9 %copy.21 = bf16[1,768,512]{2,1,0:T(8,128)(2,1)} copy(bf16[1,768,512]{2,1,0:T(8,128)(2,1)S(1)} %get-tuple-element.11) | data formatting | bytes 1572864
Async XLA Ops:
  0.6 1.6 %copy-start.3 = (bf16[32,512]{1,0:T(8,128)(2,1)S(1)}, bf16[32,512]{1,0:T(8,128)(2,1)}, u32[]{:S(2)}) copy-start(bf16[32,512]{1,0:T(8,128)(2,1)} %tokens.1) | copy-start | bytes 98308
  1.4 0.8 copy-start.5
  2.2 1.1 %copy-start = (bf16[1,512,768]{2,1,0:T(8,128)(2,1)S(1)}, bf16[1,512,768]{2,1,0:T(8,128)(2,1)}, u32[]{:S(2)}) copy-start(bf16[1,512,768]{2,1,0:T(8,128)(2,1)} %gate_hbm.1) | copy-start | bytes 2359300
  3.3 1.1 %copy-start.1 = (bf16[1,512,768]{2,1,0:T(8,128)(2,1)S(1)}, bf16[1,512,768]{2,1,0:T(8,128)(2,1)}, u32[]{:S(2)}) copy-start(bf16[1,512,768]{2,1,0:T(8,128)(2,1)} %up_hbm.1) | copy-start | bytes 2359300
  4.5 1.1 %copy-start.2 = (bf16[1,768,512]{2,1,0:T(8,128)(2,1)S(1)}, bf16[1,768,512]{2,1,0:T(8,128)(2,1)}, u32[]{:S(2)}) copy-start(bf16[1,768,512]{2,1,0:T(8,128)(2,1)} %down_hbm.1) | copy-start | bytes 2359300
  5.6 0.8 copy-start.4

commit v2 on v1

v2 whole, which is shorter than its diff:
```python
import functools

import jax
import jax.numpy as jnp
from jax import lax
from jax.experimental import pallas as pl
from jax.experimental.pallas import tpu as pltpu
from jax.sharding import PartitionSpec as P

BF = jnp.bfloat16
F32 = jnp.float32
LANES = 128
PARTS = 4


def matmul(left, right, left_dim=1, right_dim=0):
    return lax.dot_general(
        left, right, (((left_dim,), (right_dim,)), ((), ())), preferred_element_type=F32
    )


def remote(src, dst, send_sem, recv_sem, device):
    return pltpu.make_async_remote_copy(
        src_ref=src,
        dst_ref=dst,
        send_sem=send_sem,
        recv_sem=recv_sem,
        device_id=device,
        device_id_type=pl.DeviceIdType.MESH,
    )


def kernel(
    side,
    tokens_hbm, out_grad_hbm, routes_hbm, weight_hbm, placement_hbm, gate_hbm, up_hbm, down_hbm,
    in_grad_hbm, gate_grad_hbm, up_grad_hbm, down_grad_hbm,
    tokens, out_grad, routes, route_weight, placement, gate, up, down,
    in_grad, gate_grad, up_grad, down_grad,
    send0, send1, mid0, mid1, recv, rows_all, grad_all,
    psend, psum, prel, precv, full, hid, ret, rmid, fin0, fin1, wide, narrow, select,
    load_sem, store_sem, go_sem, s1_send, s1_recv, s2_send, s2_recv,
    p_send, p_recv, a_send, a_recv, h_send, h_recv, r1_send, r1_recv, r2_send, r2_recv,
):
    n = side
    block = n * n
    experts = 2 * block
    count_tok, width = tokens.shape
    chunks = width // LANES
    units = 2 * chunks
    hidden_dim = gate.shape[1]
    chosen = routes.shape[0]
    span = experts // PARTS
    me = lax.axis_index("expert")
    d = lax.axis_index("dp")
    y = me // (2 * n)
    z = lax.rem(me // 2, n)
    c = lax.rem(me, 2)

    def at(yy, zz, cc):
        return {"expert": (yy * n + zz) * 2 + cc}

    def turn(base, i):
        return lax.rem(base + i, n)

    sibling = at(y, z, 1 - c)

    loads = [
        pltpu.make_async_copy(src, dst, load_sem.at[i])
        for i, (src, dst) in enumerate(
            (
                (placement_hbm, placement), (routes_hbm, routes), (weight_hbm, route_weight),
                (tokens_hbm, tokens), (out_grad_hbm, out_grad),
                (gate_hbm.at[0], gate), (up_hbm.at[0], up), (down_hbm.at[0], down),
            )
        )
    ]
    for load in loads:
        load.start()

    barrier = pltpu.get_barrier_semaphore()
    greeted = [sibling]
    for i in range(1, n):
        for cc in range(2):
            greeted += [at(turn(y, i), z, cc), at(y, turn(z, i), cc)]
    right, left = lax.rem(d + 1, PARTS), lax.rem(d + PARTS - 1, PARTS)
    opposite = lax.rem(d + 2, PARTS)
    greeted += [{"dp": right}, {"dp": left}, {"dp": opposite}]
    for device in greeted:
        pl.semaphore_signal(
            barrier, inc=1, device_id=device, device_id_type=pl.DeviceIdType.MESH
        )
    for load in loads[:5]:
        load.wait()

    place = placement[...]
    place_y, place_z, place_c = place // (2 * n), lax.rem(place // 2, n), lax.rem(place, 2)
    spot = jnp.where(place_c == 0, place_y * n + place_z, block + place_z * n + place_y)
    spot = jnp.transpose(jnp.broadcast_to(spot.astype(F32), (LANES, experts)))[:, :count_tok]
    expert_ids = lax.broadcasted_iota(jnp.int32, (experts, count_tok), 0)
    expert_ids_f = expert_ids.astype(F32)
    named = jnp.zeros((experts, count_tok), F32)
    weight = jnp.zeros((experts, count_tok), F32)
    for k in range(chosen):
        hit = routes[k : k + 1, :] == expert_ids
        where = jnp.sum(jnp.where(hit, spot, 0.0), axis=0, keepdims=True)
        mine = where == expert_ids_f
        named = jnp.where(mine, 1.0, named)
        weight = jnp.where(mine, route_weight[k : k + 1, :], weight)
    before = (
        lax.broadcasted_iota(jnp.int32, (count_tok, count_tok), 0)
        < lax.broadcasted_iota(jnp.int32, (count_tok, count_tok), 1)
    ).astype(BF)
    rank = matmul(named.astype(BF), before)

    for r in range(2):
        chosen_rank = rank < 0.5 if r == 0 else rank > 0.5
        pick = jnp.where(chosen_rank, named, 0.0)
        select[r] = pick.astype(BF)
        row_weight = jnp.sum(pick * weight, axis=1, keepdims=True)
        token_rows = matmul(select[r], tokens[...])
        grad_rows = matmul(select[r], out_grad[...])
        for j in range(chunks):
            lanes = slice(j * LANES, (j + 1) * LANES)
            wide[pl.ds(r * units + j, experts, stride=2 * units), :] = token_rows[:, lanes]
            wide[pl.ds(r * units + chunks + j, experts, stride=2 * units), :] = (
                row_weight * grad_rows[:, lanes]
            )
    ready = wide[...].astype(BF).reshape(2, n, n, 2 * units, LANES)
    send0[...] = ready[0]
    send1[...] = ready[1]

    pl.semaphore_wait(barrier, len(greeted))

    @pl.when(c == 1)
    def _():
        pl.semaphore_wait(go_sem, 1)

    lines = ((send0, mid0, y), (send1, mid1, z))
    for i in range(1, n):
        for p, (sent, mid, base) in enumerate(lines):
            other = turn(base, i)
            device = at(other, z, c) if p == 0 else at(y, other, c)
            remote(sent.at[other], mid.at[base], s1_send.at[p], s1_recv.at[p], device).start()
    for sent, mid, base in lines:
        mid[base] = sent[base]
    if n > 1:
        most = pl.ds(0, n - 1)
        for p, (sent, mid, base) in enumerate(lines):
            remote(sent.at[most], mid.at[most], s1_send.at[p], s1_recv.at[p], sibling).wait_send()

    @pl.when(c == 0)
    def _():
        pl.semaphore_signal(
            go_sem, inc=1, device_id=sibling, device_id_type=pl.DeviceIdType.MESH
        )

    for p, (sent, mid, slot) in enumerate(lines):
        base = z if p == 0 else y
        if n > 1:
            remote(sent.at[most], mid.at[most], s1_send.at[p], s1_recv.at[p], sibling).wait_recv()
        for i in range(1, n):
            other = turn(base, i)
            device = at(y, other, 0) if p == 0 else at(other, z, 1)
            remote(
                mid.at[:, other], recv.at[c, base], s2_send, s2_recv.at[c], device
            ).start()

        @pl.when(c == p)
        def _():
            recv[c, base] = mid[:, base]

        @pl.when(c != p)
        def _():
            remote(
                mid.at[:, base], recv.at[c, base], s2_send, s2_recv.at[c], sibling
            ).start()

    half = span // 2
    first, second = pl.ds(0, half), pl.ds(half, half)

    def hop(src, dst, sems, h, i, device):
        send_sem, recv_sem = sems
        return remote(src, dst, send_sem.at[h, i], recv_sem.at[h, i], {"dp": device})

    def sums(h, i):
        src, dst, device = (
            lambda: (psend.at[h, opposite, first], prel.at[h, 0], right),
            lambda: (psend.at[h, opposite, second], prel.at[h, 1], left),
            lambda: (psend.at[h, right, second], precv.at[h, 0, second], right),
            lambda: (psend.at[h, left, first], precv.at[h, 1, first], left),
            lambda: (psum.at[h, 0], precv.at[h, 0, first], right),
            lambda: (psum.at[h, 1], precv.at[h, 1, second], left),
        )[i]()
        return hop(src, dst, (p_send, p_recv), h, i, device)

    def gathers(h, i):
        owner, part, device = (
            (d, first, right), (d, second, left), (d, second, right), (d, first, left),
            (left, first, right), (right, second, left),
        )[i]
        piece = full.at[h, owner, part]
        return hop(piece, piece, (a_send, a_recv), h, i, device)

    def gathered(h, i):
        owner, part = (
            (left, first), (right, second), (left, second), (right, first),
            (opposite, first), (opposite, second),
        )[i]
        piece = full.at[h, owner, part]
        return hop(piece, piece, (a_send, a_recv), h, i, right)

    def hidden_copy(h, i):
        owner = lax.rem(d + PARTS - i, PARTS)
        send_piece, piece = hid.at[h, d], hid.at[h, owner]
        return (
            hop(send_piece, send_piece, (h_send, h_recv), h, i - 1, lax.rem(d + i, PARTS)),
            hop(piece, piece, (h_send, h_recv), h, i - 1, lax.rem(d + i, PARTS)),
        )

    def partial_sums(h):
        for same in range(2):
            count = n - 1 if same else n
            if count:
                part = pl.ds(0, count)

                @pl.when((c == h) if same else (c != h))
                def _():
                    remote(
                        recv.at[h, part], recv.at[h, part], s2_send, s2_recv.at[h], sibling
                    ).wait_recv()

        rows = block * 2 * units
        wide[0:rows, :] = recv[h].reshape(rows, LANES).astype(F32)
        for r in range(2):
            start = h * experts + r * block
            for j in range(chunks):
                lanes = slice(j * LANES, (j + 1) * LANES)
                for kind, target in enumerate((rows_all, grad_all)):
                    offset = r * units + kind * chunks + j
                    target[start : start + block, lanes] = wide[
                        pl.ds(offset, block, stride=2 * units), :
                    ].astype(BF)
        if h == 0:
            for load in loads[5:]:
                load.wait()
        rows = slice(h * experts, (h + 1) * experts)
        shape = (PARTS, span, hidden_dim)
        psend[h, :, :, 0:hidden_dim] = (
            matmul(rows_all[rows, :], gate[...]).astype(BF).reshape(shape)
        )
        psend[h, :, :, hidden_dim : 2 * hidden_dim] = (
            matmul(rows_all[rows, :], up[...]).astype(BF).reshape(shape)
        )
        psend[h, :, :, 2 * hidden_dim :] = (
            matmul(grad_all[rows, :], down[...], 1, 1).astype(BF).reshape(shape)
        )
        for i in range(4):
            sums(h, i).start()

    def pass_sums(h):
        sums(h, 0).wait_recv()
        psum[h, 0] = (psend[h, right, first].astype(F32) + prel[h, 0].astype(F32)).astype(BF)
        sums(h, 4).start()
        sums(h, 1).wait_recv()
        psum[h, 1] = (psend[h, left, second].astype(F32) + prel[h, 1].astype(F32)).astype(BF)
        sums(h, 5).start()

    def activations(h):
        for i in range(2, 6):
            sums(h, i).wait_recv()
        total = (
            psend[h, d].astype(F32) + precv[h, 0].astype(F32) + precv[h, 1].astype(F32)
        )
        gate_sum = total[:, 0:hidden_dim]
        up_sum = total[:, hidden_dim : 2 * hidden_dim]
        hidden_grad = total[:, 2 * hidden_dim :]
        sigma = jax.nn.sigmoid(gate_sum)
        active = gate_sum * sigma
        full[h, d, :, 0:hidden_dim] = (
            hidden_grad * up_sum * sigma * (1.0 + gate_sum * (1.0 - sigma))
        ).astype(BF)
        full[h, d, :, hidden_dim:] = (hidden_grad * active).astype(BF)
        for i in range(4):
            gathers(h, i).start()
        hid[h, d] = (active * up_sum).astype(BF)

    def pass_gathers(h):
        gathered(h, 0).wait_recv()
        gathers(h, 4).start()
        gathered(h, 1).wait_recv()
        gathers(h, 5).start()

    def row_gradients(h):
        for i in range(2, 6):
            gathered(h, i).wait_recv()
        gate_back = full[h, :, :, 0:hidden_dim].reshape(experts, hidden_dim)
        up_back = full[h, :, :, hidden_dim:].reshape(experts, hidden_dim)
        row_back = matmul(gate_back, gate[...], 1, 1) + matmul(up_back, up[...], 1, 1)
        for r in range(2):
            for j in range(chunks):
                narrow[pl.ds(r * chunks + j, block, stride=units), :] = row_back[
                    r * block : (r + 1) * block, j * LANES : (j + 1) * LANES
                ]
        ret[h] = narrow[0 : block * units, :].astype(BF).reshape(n, n, units, LANES)

        base = jnp.where(c == 0, z, y)
        for i in range(n):
            other = turn(base, i)
            device = at(jnp.where(c == 0, y, other), jnp.where(c == 0, other, z), h)

            def go():
                remote(
                    ret.at[h, other], rmid.at[c, base], r1_send.at[h], r1_recv, device
                ).start()

            if i:
                go()
            else:
                pl.when(c != h)(go)

                @pl.when(c == h)
                def _():
                    rmid[c, base] = ret[h, base]

    def return_second():
        part = pl.ds(0, 2 * n - 1)
        mine = rmid.reshape(2 * n, n, units, LANES).at[part]
        remote(mine, mine, r1_send.at[0], r1_recv, sibling).wait_recv()
        for i in range(1, n):
            yy, zz = turn(y, i), turn(z, i)
            remote(
                rmid.at[0, :, yy], fin0.at[y], r2_send.at[0], r2_recv.at[0], at(yy, z, c)
            ).start()
            remote(
                rmid.at[1, :, zz], fin1.at[z], r2_send.at[1], r2_recv.at[1], at(y, zz, c)
            ).start()
        fin0[y] = rmid[0, :, y]
        fin1[z] = rmid[1, :, z]

    partial_sums(0)
    pass_sums(0)
    partial_sums(1)
    activations(0)
    pass_sums(1)
    pass_gathers(0)
    activations(1)
    pass_gathers(1)
    row_gradients(0)
    for h in range(2):
        for i in range(1, PARTS):
            hidden_copy(h, i)[0].start()
    row_gradients(1)
    pl.when(c == 0)(return_second)

    stores = []

    def store(i, src, dst):
        stores.append(pltpu.make_async_copy(src, dst, store_sem.at[i]))
        stores[-1].start()

    def weight_gradient(part, result, out):
        back = full[:, :, :, part * hidden_dim : (part + 1) * hidden_dim]
        back = back.reshape(2 * experts, hidden_dim)
        result[...] = matmul(rows_all[...], back, 0, 0).astype(BF)
        store(part, result, out.at[0])

    weight_gradient(0, gate_grad, gate_grad_hbm)
    pl.when(c == 1)(return_second)
    weight_gradient(1, up_grad, up_grad_hbm)
    for h in range(2):
        for i in range(1, PARTS):
            hidden_copy(h, i)[1].wait()
    hidden = hid[...].reshape(2 * experts, hidden_dim)
    down_grad[...] = matmul(hidden, grad_all[...], 0, 0).astype(BF)
    store(2, down_grad, down_grad_hbm.at[0])

    for h in range(2):
        for i in range(6):
            sums(h, i).wait_send()
            gathers(h, i).wait_send()
    for same in range(2):
        count = n - 1 if same else n
        for h in range(2):
            if count:
                part = pl.ds(0, count)

                @pl.when((c == h) if same else (c != h))
                def _():
                    remote(
                        ret.at[h, part], ret.at[h, part], r1_send.at[h], r1_recv, sibling
                    ).wait_send()

    part = pl.ds(0, 2 * n - 1)
    moved = recv.reshape(2 * n, n, 2 * units, LANES).at[part]
    remote(moved, moved, s2_send, s2_recv.at[0], sibling).wait_send()

    if n > 1:
        for p, fin in enumerate((fin0, fin1)):
            remote(fin.at[most], fin.at[most], r2_send.at[p], r2_recv.at[p], sibling).wait()
    whole = block * units
    narrow[0:whole, :] = fin0[...].reshape(whole, LANES).astype(F32)
    narrow[whole : 2 * whole, :] = fin1[...].reshape(whole, LANES).astype(F32)
    for j in range(chunks):
        total = jnp.zeros((count_tok, LANES), F32)
        for r in range(2):
            came = narrow[pl.ds(r * chunks + j, experts, stride=units), :].astype(BF)
            total = total + matmul(select[r], came, 0, 0)
        in_grad[:, j * LANES : (j + 1) * LANES] = total.astype(BF)
    store(3, in_grad, in_grad_hbm)
    for copy in stores:
        copy.wait()


def hand_over(*refs):
    count = (len(refs) - 2) // 3
    given, kept, passed = refs[:count], refs[count : 2 * count], refs[2 * count : 3 * count]
    come, go = refs[-2:]
    pieces = []
    for i in range(count):
        rows = given[i].shape[-2]
        step = max(rows // 4, min(rows, 32))
        for at in range(0, rows, step):
            part = (0, pl.ds(at, step)) if len(given[i].shape) == 3 else (pl.ds(at, step),)
            pieces.append((given[i].at[part], passed[i].at[part], kept[i].at[part]))
    reads = [pltpu.make_async_copy(src, mid, come.at[k]) for k, (src, mid, _) in enumerate(pieces)]
    writes = [pltpu.make_async_copy(mid, dst, go.at[k]) for k, (_, mid, dst) in enumerate(pieces)]
    for read in reads:
        read.start()
    for read, write in zip(reads, writes):
        read.wait()
        write.start()
    for write in writes:
        write.wait()


def local(tokens, out_grad, routes, route_weight, placement, gate_weight, up_weight, down_weight):
    experts = lax.axis_size("expert")
    side = 1
    while 2 * side * side < experts:
        side *= 2
    n = side
    count_tok, width = tokens.shape
    chosen = routes.shape[1]
    _, _, hidden_dim = gate_weight.shape
    units = 2 * width // LANES
    span = experts // PARTS
    hbm = pl.BlockSpec(memory_space=pltpu.HBM)
    dma = pltpu.SemaphoreType.DMA

    def buf(*shape, dtype=BF):
        return pltpu.VMEM(shape, dtype)

    shapes = (
        jax.ShapeDtypeStruct((count_tok, width), BF),
        jax.ShapeDtypeStruct(gate_weight.shape, BF),
        jax.ShapeDtypeStruct(up_weight.shape, BF),
        jax.ShapeDtypeStruct(down_weight.shape, BF),
    )
    results = pl.pallas_call(
        functools.partial(kernel, side),
        out_shape=shapes,
        in_specs=[hbm] * 8,
        out_specs=(hbm,) * 4,
        scratch_shapes=[
            buf(count_tok, width), buf(count_tok, width),
            buf(chosen, count_tok, dtype=jnp.int32), buf(chosen, count_tok, dtype=F32),
            buf(1, experts, dtype=jnp.int32),
            buf(width, hidden_dim), buf(width, hidden_dim), buf(hidden_dim, width),
            buf(count_tok, width),
            buf(width, hidden_dim), buf(width, hidden_dim), buf(hidden_dim, width),
            buf(n, n, 2 * units, LANES), buf(n, n, 2 * units, LANES),
            buf(n, n, 2 * units, LANES), buf(n, n, 2 * units, LANES),
            buf(2, n, n, 2 * units, LANES),
            buf(2 * experts, width), buf(2 * experts, width),
            buf(2, PARTS, span, 3 * hidden_dim),
            buf(2, 2, span // 2, 3 * hidden_dim),
            buf(2, 2, span // 2, 3 * hidden_dim),
            buf(2, 2, span, 3 * hidden_dim),
            buf(2, PARTS, span, 2 * hidden_dim),
            buf(2, PARTS, span, hidden_dim),
            buf(2, n, n, units, LANES), buf(2, n, n, units, LANES),
            buf(n, n, units, LANES), buf(n, n, units, LANES),
            buf(experts * 2 * units, LANES, dtype=F32),
            buf(experts * units, LANES, dtype=F32),
            buf(2, experts, count_tok),
            dma((8,)), dma((4,)), pltpu.SemaphoreType.REGULAR,
            dma((2,)), dma((2,)), dma, dma((2,)),
            dma((2, 6)), dma((2, 6)), dma((2, 6)), dma((2, 6)), dma((2, 3)), dma((2, 3)),
            dma((2,)), dma, dma((2,)), dma((2,)),
        ],
        compiler_params=pltpu.CompilerParams(
            collective_id=0, has_side_effects=True, vmem_limit_bytes=61 << 20
        ),
        name="expert_backward",
    )(
        tokens, out_grad, routes.T, route_weight.T, placement.reshape(1, experts),
        gate_weight, up_weight, down_weight,
    )
    return pl.pallas_call(
        hand_over,
        out_shape=shapes,
        in_specs=[hbm] * 4,
        out_specs=(hbm,) * 4,
        scratch_shapes=[buf(*shape.shape) for shape in shapes] + [dma((16,)), dma((16,))],
        compiler_params=pltpu.CompilerParams(vmem_limit_bytes=61 << 20),
        name="hand_over",
    )(*results)


def solution(mesh):
    in_specs = (
        P("expert", "dp"),
        P("expert", "dp"),
        P("expert", None),
        P("expert", None),
        P(),
        P("expert", "dp", None),
        P("expert", "dp", None),
        P("expert", None, "dp"),
    )
    out_specs = (
        P("expert", "dp"),
        P("expert", "dp", None),
        P("expert", "dp", None),
        P("expert", None, "dp"),
    )
    return jax.shard_map(local, mesh=mesh, in_specs=in_specs, out_specs=out_specs, check_vma=False)
```

time: 80.8 us -> 69.3 us (0.86)
  local copies, waits for them, and re-layouts: 8.96 us -> 0 us
  Pallas kernels: 70.4 us -> 68.5 us
    unnamed x18 -> x0, local copies, waits for them, and re-layouts: 8.96 us -> none
    pallas_call x1 -> x2, Pallas kernels: 70.4 us -> 68.5 us  [the longest x1 65.8 us: local(): pl.pallas_call(functools.partial(kernel, side), out_shape=shapes, in_spec...]
where the time goes in v2:
time: 69.3 us; the launch traced here: 69.1 us
  Pallas kernels  68.5 us (99%)
    pallas_call x1, Pallas kernels, local(): pl.pallas_call(functools.partial(kernel, side), out_shape=shapes, in_spec...  65.8 us
    pallas_call x1, Pallas kernels, local(): pl.pallas_call(hand_over, out_shape=shapes, in_specs=[hbm] * 4, out_specs...  2.71 us

profile of v2, /device:TPU:1, one launch (start us, length us, event | category | flops | bytes accessed | tf_op | source)
XLA Modules:
  0.0 69.1 jit_solution(4633203449971836193)
XLA Ops:
  0.6 65.8 %expert_backward.1 = (bf16[32,512]{1,0:T(8,128)(2,1)}, bf16[1,512,768]{2,1,0:T(8,128)(2,1)}, bf16[1,512,768]{2,1,0:T(8,128)(2,1)}, bf16[1,768,512]{2,1,0:T(8,128)(2,1)}) custom-call(bf16[32,512]{1,0:T(8,128)(2,1)} %tokens_hbm.1, bf16[32,512]{1,0:T(8,128)(2,1)} %out_grad_hbm.1, s32[8,32]{1,0:T(8,128)} %bitcast.3, f32[8,32]{1,0:T(8,128)} %bitcast.4, ...), custom_call_target="tpu_custom_call" | custom-call | tf_op jit(solution)/shard_map/expert_backward/pallas_call | solution.py:459
  66.4 2.7 %hand_over.1 = (bf16[32,512]{1,0:T(8,128)(2,1)}, bf16[1,512,768]{2,1,0:T(8,128)(2,1)}, bf16[1,512,768]{2,1,0:T(8,128)(2,1)}, bf16[1,768,512]{2,1,0:T(8,128)(2,1)}) custom-call(bf16[32,512]{1,0:T(8,128)(2,1)} %get-tuple-element.8.refs_0_, bf16[1,512,768]{2,1,0:T(8,128)(2,1)} %get-tuple-element.9.refs_1_, bf16[1,512,768]{2,1,0:T(8,128)(2,1)} %get-tuple-element.10.refs_2_, ...), custom_call_target="tpu_custom_call" | custom-call | tf_op jit(solution)/shard_map/hand_over/pallas_call | solution.py:499

commit v3 on v2

--- a/solution.py
+++ b/solution.py
@@ -37,9 +37,9 @@
     tokens, out_grad, routes, route_weight, placement, gate, up, down,
     in_grad, gate_grad, up_grad, down_grad,
     send0, send1, mid0, mid1, recv, rows_all, grad_all,
-    psend, psum, prel, precv, full, hid, ret, rmid, fin0, fin1, wide, narrow, select,
+    turned, psend, psum, prel, precv, full, hid, ret, fin, wide, narrow, select,
     load_sem, store_sem, go_sem, s1_send, s1_recv, s2_send, s2_recv,
-    p_send, p_recv, a_send, a_recv, h_send, h_recv, r1_send, r1_recv, r2_send, r2_recv,
+    p_send, p_recv, a_send, a_recv, h_send, h_recv, r_send, r_recv,
 ):
     n = side
     block = n * n
@@ -60,7 +60,9 @@
         return {"expert": (yy * n + zz) * 2 + cc}
 
     def turn(base, i):
-        return lax.rem(base + i, n)
+        return jnp.bitwise_and(base + i, n - 1)
+
+    offsets = sorted(range(n), key=lambda i: (-min(i, n - i), i))
 
     sibling = at(y, z, 1 - c)
 
@@ -136,7 +138,7 @@
         pl.semaphore_wait(go_sem, 1)
 
     lines = ((send0, mid0, y), (send1, mid1, z))
-    for i in range(1, n):
+    for i in offsets[:-1]:
         for p, (sent, mid, base) in enumerate(lines):
             other = turn(base, i)
             device = at(other, z, c) if p == 0 else at(y, other, c)
@@ -158,21 +160,24 @@
         base = z if p == 0 else y
         if n > 1:
             remote(sent.at[most], mid.at[most], s1_send.at[p], s1_recv.at[p], sibling).wait_recv()
-        for i in range(1, n):
+        for i in range(n):
+            for j in range(n):
+                turned[p, i, j] = mid[j, i]
+        for i in offsets[:-1]:
             other = turn(base, i)
             device = at(y, other, 0) if p == 0 else at(other, z, 1)
             remote(
-                mid.at[:, other], recv.at[c, base], s2_send, s2_recv.at[c], device
+                turned.at[p, other], recv.at[c, base], s2_send, s2_recv.at[c], device
             ).start()
 
         @pl.when(c == p)
         def _():
-            recv[c, base] = mid[:, base]
+            recv[c, base] = turned[p, base]
 
         @pl.when(c != p)
         def _():
             remote(
-                mid.at[:, base], recv.at[c, base], s2_send, s2_recv.at[c], sibling
+                turned.at[p, base], recv.at[c, base], s2_send, s2_recv.at[c], sibling
             ).start()
 
     half = span // 2
@@ -303,39 +308,26 @@
                 ]
         ret[h] = narrow[0 : block * units, :].astype(BF).reshape(n, n, units, LANES)
 
-        base = jnp.where(c == 0, z, y)
-        for i in range(n):
-            other = turn(base, i)
-            device = at(jnp.where(c == 0, y, other), jnp.where(c == 0, other, z), h)
-
-            def go():
-                remote(
-                    ret.at[h, other], rmid.at[c, base], r1_send.at[h], r1_recv, device
-                ).start()
-
-            if i:
-                go()
-            else:
-                pl.when(c != h)(go)
-
-                @pl.when(c == h)
-                def _():
-                    rmid[c, base] = ret[h, base]
-
-    def return_second():
-        part = pl.ds(0, 2 * n - 1)
-        mine = rmid.reshape(2 * n, n, units, LANES).at[part]
-        remote(mine, mine, r1_send.at[0], r1_recv, sibling).wait_recv()
-        for i in range(1, n):
-            yy, zz = turn(y, i), turn(z, i)
-            remote(
-                rmid.at[0, :, yy], fin0.at[y], r2_send.at[0], r2_recv.at[0], at(yy, z, c)
-            ).start()
-            remote(
-                rmid.at[1, :, zz], fin1.at[z], r2_send.at[1], r2_recv.at[1], at(y, zz, c)
-            ).start()
-        fin0[y] = rmid[0, :, y]
-        fin1[z] = rmid[1, :, z]
+    def give_back(h):
+        along, across = jnp.where(c == 0, z, y), jnp.where(c == 0, y, z)
+        slots = [turn(along, i) for i in offsets]
+        others = [turn(across, i) for i in offsets]
+        to_slot = [slot * jnp.where(c == 0, 2, 2 * n) + h for slot in slots]
+        to_other = [other * jnp.where(c == 0, 2 * n, 2) for other in others]
+        for i, slot in enumerate(slots):
+            for k, other in enumerate(others):
+                copy = remote(
+                    ret.at[h, slot, other], fin.at[c, across, along], r_send.at[h], r_recv,
+                    {"expert": to_slot[i] + to_other[k]},
+                )
+                if offsets[i] or offsets[k]:
+                    copy.start()
+                else:
+                    pl.when(c != h)(copy.start)
+
+        @pl.when(c == h)
+        def _():
+            fin[c, across, along] = ret[h, along, across]
 
     partial_sums(0)
     pass_sums(0)
@@ -344,13 +336,14 @@
     pass_sums(1)
     pass_gathers(0)
     activations(1)
+    row_gradients(0)
     pass_gathers(1)
-    row_gradients(0)
+    give_back(0)
+    row_gradients(1)
+    give_back(1)
     for h in range(2):
         for i in range(1, PARTS):
             hidden_copy(h, i)[0].start()
-    row_gradients(1)
-    pl.when(c == 0)(return_second)
 
     stores = []
 
@@ -365,7 +358,6 @@
         store(part, result, out.at[0])
 
     weight_gradient(0, gate_grad, gate_grad_hbm)
-    pl.when(c == 1)(return_second)
     weight_gradient(1, up_grad, up_grad_hbm)
     for h in range(2):
         for i in range(1, PARTS):
@@ -378,28 +370,24 @@
         for i in range(6):
             sums(h, i).wait_send()
             gathers(h, i).wait_send()
+    pieces = fin.reshape(experts, units, LANES)
     for same in range(2):
-        count = n - 1 if same else n
+        count = block - 1 if same else block
         for h in range(2):
             if count:
-                part = pl.ds(0, count)
+                part = pieces.at[pl.ds(0, count)]
 
                 @pl.when((c == h) if same else (c != h))
                 def _():
-                    remote(
-                        ret.at[h, part], ret.at[h, part], r1_send.at[h], r1_recv, sibling
-                    ).wait_send()
+                    remote(part, part, r_send.at[h], r_recv, sibling).wait_send()
 
     part = pl.ds(0, 2 * n - 1)
     moved = recv.reshape(2 * n, n, 2 * units, LANES).at[part]
     remote(moved, moved, s2_send, s2_recv.at[0], sibling).wait_send()
 
-    if n > 1:
-        for p, fin in enumerate((fin0, fin1)):
-            remote(fin.at[most], fin.at[most], r2_send.at[p], r2_recv.at[p], sibling).wait()
-    whole = block * units
-    narrow[0:whole, :] = fin0[...].reshape(whole, LANES).astype(F32)
-    narrow[whole : 2 * whole, :] = fin1[...].reshape(whole, LANES).astype(F32)
+    part = pieces.at[pl.ds(0, experts - 1)]
+    remote(part, part, r_send.at[0], r_recv, sibling).wait_recv()
+    narrow[...] = fin[...].reshape(experts * units, LANES).astype(F32)
     for j in range(chunks):
         total = jnp.zeros((count_tok, LANES), F32)
         for r in range(2):
@@ -472,6 +460,7 @@
             buf(n, n, 2 * units, LANES), buf(n, n, 2 * units, LANES),
             buf(2, n, n, 2 * units, LANES),
             buf(2 * experts, width), buf(2 * experts, width),
+            buf(2, n, n, 2 * units, LANES),
             buf(2, PARTS, span, 3 * hidden_dim),
             buf(2, 2, span // 2, 3 * hidden_dim),
             buf(2, 2, span // 2, 3 * hidden_dim),
@@ -479,14 +468,13 @@
             buf(2, PARTS, span, 2 * hidden_dim),
             buf(2, PARTS, span, hidden_dim),
             buf(2, n, n, units, LANES), buf(2, n, n, units, LANES),
-            buf(n, n, units, LANES), buf(n, n, units, LANES),
             buf(experts * 2 * units, LANES, dtype=F32),
             buf(experts * units, LANES, dtype=F32),
             buf(2, experts, count_tok),
             dma((8,)), dma((4,)), pltpu.SemaphoreType.REGULAR,
             dma((2,)), dma((2,)), dma, dma((2,)),
             dma((2, 6)), dma((2, 6)), dma((2, 6)), dma((2, 6)), dma((2, 3)), dma((2, 3)),
-            dma((2,)), dma, dma((2,)), dma((2,)),
+            dma((2,)), dma,
         ],
         compiler_params=pltpu.CompilerParams(
             collective_id=0, has_side_effects=True, vmem_limit_bytes=61 << 20

time: 69.3 us -> 64.8 us (0.935)
  Pallas kernels: 68.5 us -> 64 us
    pallas_call x1, Pallas kernels: 65.8 us -> 61.3 us  [local(): pl.pallas_call(functools.partial(kernel, side), out_shape=shapes, in_spec...]
where the time goes in v3:
time: 64.8 us; the launch traced here: 64.6 us
  Pallas kernels  64 us (99%)
    pallas_call x1, Pallas kernels, local(): pl.pallas_call(functools.partial(kernel, side), out_shape=shapes, in_spec...  61.3 us
    pallas_call x1, Pallas kernels, local(): pl.pallas_call(hand_over, out_shape=shapes, in_specs=[hbm] * 4, out_specs...  2.71 us

profile of v3, /device:TPU:1, one launch (start us, length us, event | category | flops | bytes accessed | tf_op | source)
XLA Modules:
  0.0 64.6 jit_solution(15044094658319877473)
XLA Ops:
  0.6 61.3 %expert_backward.1 = (bf16[32,512]{1,0:T(8,128)(2,1)}, bf16[1,512,768]{2,1,0:T(8,128)(2,1)}, bf16[1,512,768]{2,1,0:T(8,128)(2,1)}, bf16[1,768,512]{2,1,0:T(8,128)(2,1)}) custom-call(bf16[32,512]{1,0:T(8,128)(2,1)} %tokens_hbm.1, bf16[32,512]{1,0:T(8,128)(2,1)} %out_grad_hbm.1, s32[8,32]{1,0:T(8,128)} %bitcast.3, f32[8,32]{1,0:T(8,128)} %bitcast.4, ...), custom_call_target="tpu_custom_call" | custom-call | tf_op jit(solution)/shard_map/expert_backward/pallas_call | solution.py:447
  61.9 2.7 %hand_over.1 = (bf16[32,512]{1,0:T(8,128)(2,1)}, bf16[1,512,768]{2,1,0:T(8,128)(2,1)}, bf16[1,512,768]{2,1,0:T(8,128)(2,1)}, bf16[1,768,512]{2,1,0:T(8,128)(2,1)}) custom-call(bf16[32,512]{1,0:T(8,128)(2,1)} %get-tuple-element.8.refs_0_, bf16[1,512,768]{2,1,0:T(8,128)(2,1)} %get-tuple-element.9.refs_1_, bf16[1,512,768]{2,1,0:T(8,128)(2,1)} %get-tuple-element.10.refs_2_, ...), custom_call_target="tpu_custom_call" | custom-call | tf_op jit(solution)/shard_map/hand_over/pallas_call | solution.py:487

commit v4 on v3

--- a/solution.py
+++ b/solution.py
@@ -38,7 +38,7 @@
     in_grad, gate_grad, up_grad, down_grad,
     send0, send1, mid0, mid1, recv, rows_all, grad_all,
     turned, psend, psum, prel, precv, full, hid, ret, fin, wide, narrow, select,
-    load_sem, store_sem, go_sem, s1_send, s1_recv, s2_send, s2_recv,
+    load_sem, store_sem, s1_send, s1_recv, s2_send, s2_recv,
     p_send, p_recv, a_send, a_recv, h_send, h_recv, r_send, r_recv,
 ):
     n = side
@@ -49,7 +49,7 @@
     units = 2 * chunks
     hidden_dim = gate.shape[1]
     chosen = routes.shape[0]
-    span = experts // PARTS
+    span = block // PARTS
     me = lax.axis_index("expert")
     d = lax.axis_index("dp")
     y = me // (2 * n)
@@ -114,7 +114,9 @@
     ).astype(BF)
     rank = matmul(named.astype(BF), before)
 
-    for r in range(2):
+    lines = ((send0, mid0, y), (send1, mid1, z))
+
+    def prepare(r):
         chosen_rank = rank < 0.5 if r == 0 else rank > 0.5
         pick = jnp.where(chosen_rank, named, 0.0)
         select[r] = pick.astype(BF)
@@ -123,96 +125,103 @@
         grad_rows = matmul(select[r], out_grad[...])
         for j in range(chunks):
             lanes = slice(j * LANES, (j + 1) * LANES)
-            wide[pl.ds(r * units + j, experts, stride=2 * units), :] = token_rows[:, lanes]
-            wide[pl.ds(r * units + chunks + j, experts, stride=2 * units), :] = (
-                row_weight * grad_rows[:, lanes]
-            )
-    ready = wide[...].astype(BF).reshape(2, n, n, 2 * units, LANES)
-    send0[...] = ready[0]
-    send1[...] = ready[1]
-
+            wide[r, pl.ds(j, experts, stride=units), :] = token_rows[:, lanes]
+            wide[r, pl.ds(chunks + j, experts, stride=units), :] = row_weight * grad_rows[:, lanes]
+        ready = wide[r].astype(BF).reshape(2, n, n, units, LANES)
+        send0[r] = ready[0]
+        send1[r] = ready[1]
+
+    def first_stage(r):
+        for i in offsets[:-1]:
+            for p, (sent, mid, base) in enumerate(lines):
+                other = turn(base, i)
+                device = at(other, z, c) if p == 0 else at(y, other, c)
+                remote(
+                    sent.at[r, other], mid.at[r, base], s1_send.at[r, p], s1_recv.at[r, p], device
+                ).start()
+        for sent, mid, base in lines:
+            mid[r, base] = sent[r, base]
+
+    def first_copy(r, p):
+        sent, mid, _ = lines[p]
+        most = pl.ds(0, n - 1)
+        return remote(
+            sent.at[r, most], mid.at[r, most], s1_send.at[r, p], s1_recv.at[r, p], sibling
+        )
+
+    def second_stage(r):
+        group = 2 * c + r
+        for p, (sent, mid, slot) in enumerate(lines):
+            base = z if p == 0 else y
+            first_copy(r, p).wait_recv()
+            for i in range(n):
+                for j in range(n):
+                    turned[r, p, i, j] = mid[r, j, i]
+            for i in offsets[:-1]:
+                other = turn(base, i)
+                device = at(y, other, 0) if p == 0 else at(other, z, 1)
+                remote(
+                    turned.at[r, p, other], recv.at[group, base], s2_send, s2_recv.at[group], device
+                ).start()
+
+            @pl.when(c == p)
+            def _():
+                recv[group, base] = turned[r, p, base]
+
+            @pl.when(c != p)
+            def _():
+                remote(
+                    turned.at[r, p, base], recv.at[group, base], s2_send, s2_recv.at[group], sibling
+                ).start()
+
+    prepare(0)
     pl.semaphore_wait(barrier, len(greeted))
 
-    @pl.when(c == 1)
-    def _():
-        pl.semaphore_wait(go_sem, 1)
-
-    lines = ((send0, mid0, y), (send1, mid1, z))
-    for i in offsets[:-1]:
-        for p, (sent, mid, base) in enumerate(lines):
-            other = turn(base, i)
-            device = at(other, z, c) if p == 0 else at(y, other, c)
-            remote(sent.at[other], mid.at[base], s1_send.at[p], s1_recv.at[p], device).start()
-    for sent, mid, base in lines:
-        mid[base] = sent[base]
-    if n > 1:
-        most = pl.ds(0, n - 1)
-        for p, (sent, mid, base) in enumerate(lines):
-            remote(sent.at[most], mid.at[most], s1_send.at[p], s1_recv.at[p], sibling).wait_send()
-
-    @pl.when(c == 0)
-    def _():
-        pl.semaphore_signal(
-            go_sem, inc=1, device_id=sibling, device_id_type=pl.DeviceIdType.MESH
-        )
-
-    for p, (sent, mid, slot) in enumerate(lines):
-        base = z if p == 0 else y
-        if n > 1:
-            remote(sent.at[most], mid.at[most], s1_send.at[p], s1_recv.at[p], sibling).wait_recv()
-        for i in range(n):
-            for j in range(n):
-                turned[p, i, j] = mid[j, i]
-        for i in offsets[:-1]:
-            other = turn(base, i)
-            device = at(y, other, 0) if p == 0 else at(other, z, 1)
-            remote(
-                turned.at[p, other], recv.at[c, base], s2_send, s2_recv.at[c], device
-            ).start()
-
-        @pl.when(c == p)
-        def _():
-            recv[c, base] = turned[p, base]
-
-        @pl.when(c != p)
-        def _():
-            remote(
-                turned.at[p, base], recv.at[c, base], s2_send, s2_recv.at[c], sibling
-            ).start()
-
-    half = span // 2
-    first, second = pl.ds(0, half), pl.ds(half, half)
+    first_stage(0)
+    prepare(1)
+    first_stage(1)
+    for r in range(2):
+        for p in range(2):
+            first_copy(r, p).wait_send()
+
+    second_stage(0)
+    second_stage(1)
+
+    triple, double = 3 * hidden_dim, 2 * hidden_dim
+    first3, second3 = pl.ds(0, triple // 2), pl.ds(triple // 2, triple // 2)
+    first2, second2 = pl.ds(0, hidden_dim), pl.ds(hidden_dim, hidden_dim)
+    every = pl.ds(0, span)
 
     def hop(src, dst, sems, h, i, device):
         send_sem, recv_sem = sems
         return remote(src, dst, send_sem.at[h, i], recv_sem.at[h, i], {"dp": device})
 
-    def sums(h, i):
+    def sums(g, i):
         src, dst, device = (
-            lambda: (psend.at[h, opposite, first], prel.at[h, 0], right),
-            lambda: (psend.at[h, opposite, second], prel.at[h, 1], left),
-            lambda: (psend.at[h, right, second], precv.at[h, 0, second], right),
-            lambda: (psend.at[h, left, first], precv.at[h, 1, first], left),
-            lambda: (psum.at[h, 0], precv.at[h, 0, first], right),
-            lambda: (psum.at[h, 1], precv.at[h, 1, second], left),
+            lambda: (psend.at[g, opposite, every, first3], prel.at[g, 0], right),
+            lambda: (psend.at[g, opposite, every, second3], prel.at[g, 1], left),
+            lambda: (psend.at[g, right, every, second3], precv.at[g, 0, every, second3], right),
+            lambda: (psend.at[g, left, every, first3], precv.at[g, 1, every, first3], left),
+            lambda: (psum.at[g, 0], precv.at[g, 0, every, first3], right),
+            lambda: (psum.at[g, 1], precv.at[g, 1, every, second3], left),
         )[i]()
-        return hop(src, dst, (p_send, p_recv), h, i, device)
-
-    def gathers(h, i):
+        return hop(src, dst, (p_send, p_recv), g, i, device)
+
+    def gathers(g, i):
         owner, part, device = (
-            (d, first, right), (d, second, left), (d, second, right), (d, first, left),
-            (left, first, right), (right, second, left),
+            (d, first2, right), (d, second2, left), (d, second2, right), (d, first2, left),
+            (left, first2, right), (right, second2, left),
         )[i]
-        piece = full.at[h, owner, part]
-        return hop(piece, piece, (a_send, a_recv), h, i, device)
-
-    def gathered(h, i):
+        piece = full.at[g, owner, every, part]
+        return hop(piece, piece, (a_send, a_recv), g, i, device)
+
+    def gathered(g, i):
         owner, part = (
-            (left, first), (right, second), (left, second), (right, first),
-            (opposite, first), (opposite, second),
+            (left, first2), (right, second2), (left, second2), (right, first2),
+            (opposite, first2), (opposite, second2),
         )[i]
-        piece = full.at[h, owner, part]
-        return hop(piece, piece, (a_send, a_recv), h, i, right)
+        piece = full.at[g, owner, every, part]
+        return hop(piece, piece, (a_send, a_recv), g, i, right)
 
     def hidden_copy(h, i):
         owner = lax.rem(d + PARTS - i, PARTS)
@@ -222,84 +231,85 @@
             hop(piece, piece, (h_send, h_recv), h, i - 1, lax.rem(d + i, PARTS)),
         )
 
-    def partial_sums(h):
+    def partial_sums(g):
         for same in range(2):
             count = n - 1 if same else n
             if count:
-                part = pl.ds(0, count)
-
-                @pl.when((c == h) if same else (c != h))
+                part = recv.at[g, pl.ds(0, count)]
+
+                @pl.when((c == g // 2) if same else (c != g // 2))
                 def _():
-                    remote(
-                        recv.at[h, part], recv.at[h, part], s2_send, s2_recv.at[h], sibling
-                    ).wait_recv()
-
-        rows = block * 2 * units
-        wide[0:rows, :] = recv[h].reshape(rows, LANES).astype(F32)
-        for r in range(2):
-            start = h * experts + r * block
-            for j in range(chunks):
-                lanes = slice(j * LANES, (j + 1) * LANES)
-                for kind, target in enumerate((rows_all, grad_all)):
-                    offset = r * units + kind * chunks + j
-                    target[start : start + block, lanes] = wide[
-                        pl.ds(offset, block, stride=2 * units), :
-                    ].astype(BF)
-        if h == 0:
+                    remote(part, part, s2_send, s2_recv.at[g], sibling).wait_recv()
+
+        came = block * units
+        wide[g % 2, 0:came, :] = recv[g].reshape(came, LANES).astype(F32)
+        rows = slice(g * block, (g + 1) * block)
+        for j in range(chunks):
+            lanes = slice(j * LANES, (j + 1) * LANES)
+            for kind, target in enumerate((rows_all, grad_all)):
+                target[rows, lanes] = wide[
+                    g % 2, pl.ds(kind * chunks + j, block, stride=units), :
+                ].astype(BF)
+        if g == 0:
             for load in loads[5:]:
                 load.wait()
-        rows = slice(h * experts, (h + 1) * experts)
         shape = (PARTS, span, hidden_dim)
-        psend[h, :, :, 0:hidden_dim] = (
+        psend[g, :, :, 0:hidden_dim] = (
             matmul(rows_all[rows, :], gate[...]).astype(BF).reshape(shape)
         )
-        psend[h, :, :, hidden_dim : 2 * hidden_dim] = (
+        psend[g, :, :, hidden_dim:double] = (
             matmul(rows_all[rows, :], up[...]).astype(BF).reshape(shape)
         )
-        psend[h, :, :, 2 * hidden_dim :] = (
+        psend[g, :, :, double:] = (
             matmul(grad_all[rows, :], down[...], 1, 1).astype(BF).reshape(shape)
         )
         for i in range(4):
-            sums(h, i).start()
-
-    def pass_sums(h):
-        sums(h, 0).wait_recv()
-        psum[h, 0] = (psend[h, right, first].astype(F32) + prel[h, 0].astype(F32)).astype(BF)
-        sums(h, 4).start()
-        sums(h, 1).wait_recv()
-        psum[h, 1] = (psend[h, left, second].astype(F32) + prel[h, 1].astype(F32)).astype(BF)
-        sums(h, 5).start()
-
-    def activations(h):
+            sums(g, i).start()
+
+    def pass_sums(g):
+        middle = triple // 2
+        sums(g, 0).wait_recv()
+        psum[g, 0] = (
+            psend[g, right, :, 0:middle].astype(F32) + prel[g, 0].astype(F32)
+        ).astype(BF)
+        sums(g, 4).start()
+        sums(g, 1).wait_recv()
+        psum[g, 1] = (
+            psend[g, left, :, middle:].astype(F32) + prel[g, 1].astype(F32)
+        ).astype(BF)
+        sums(g, 5).start()
+
+    def activations(g):
         for i in range(2, 6):
-            sums(h, i).wait_recv()
+            sums(g, i).wait_recv()
         total = (
-            psend[h, d].astype(F32) + precv[h, 0].astype(F32) + precv[h, 1].astype(F32)
+            psend[g, d].astype(F32) + precv[g, 0].astype(F32) + precv[g, 1].astype(F32)
         )
         gate_sum = total[:, 0:hidden_dim]
-        up_sum = total[:, hidden_dim : 2 * hidden_dim]
-        hidden_grad = total[:, 2 * hidden_dim :]
+        up_sum = total[:, hidden_dim:double]
+        hidden_grad = total[:, double:]
         sigma = jax.nn.sigmoid(gate_sum)
         active = gate_sum * sigma
-        full[h, d, :, 0:hidden_dim] = (
+        full[g, d, :, 0:hidden_dim] = (
             hidden_grad * up_sum * sigma * (1.0 + gate_sum * (1.0 - sigma))
         ).astype(BF)
-        full[h, d, :, hidden_dim:] = (hidden_grad * active).astype(BF)
+        full[g, d, :, hidden_dim:] = (hidden_grad * active).astype(BF)
         for i in range(4):
-            gathers(h, i).start()
-        hid[h, d] = (active * up_sum).astype(BF)
-
-    def pass_gathers(h):
-        gathered(h, 0).wait_recv()
-        gathers(h, 4).start()
-        gathered(h, 1).wait_recv()
-        gathers(h, 5).start()
+            gathers(g, i).start()
+        hid[g, d] = (active * up_sum).astype(BF)
+
+    def pass_gathers(g):
+        gathered(g, 0).wait_recv()
+        gathers(g, 4).start()
+        gathered(g, 1).wait_recv()
+        gathers(g, 5).start()
 
     def row_gradients(h):
-        for i in range(2, 6):
-            gathered(h, i).wait_recv()
-        gate_back = full[h, :, :, 0:hidden_dim].reshape(experts, hidden_dim)
-        up_back = full[h, :, :, hidden_dim:].reshape(experts, hidden_dim)
+        for g in (2 * h, 2 * h + 1):
+            for i in range(2, 6):
+                gathered(g, i).wait_recv()
+        back = full[2 * h : 2 * h + 2].reshape(experts, double)
+        gate_back, up_back = back[:, 0:hidden_dim], back[:, hidden_dim:]
         row_back = matmul(gate_back, gate[...], 1, 1) + matmul(up_back, up[...], 1, 1)
         for r in range(2):
             for j in range(chunks):
@@ -330,20 +340,28 @@
             fin[c, across, along] = ret[h, along, across]
 
     partial_sums(0)
+    partial_sums(2)
+    partial_sums(1)
+    partial_sums(3)
     pass_sums(0)
-    partial_sums(1)
+    pass_sums(2)
+    pass_sums(1)
+    pass_sums(3)
     activations(0)
-    pass_sums(1)
+    activations(2)
+    activations(1)
+    activations(3)
     pass_gathers(0)
-    activations(1)
+    pass_gathers(2)
+    pass_gathers(1)
+    pass_gathers(3)
     row_gradients(0)
-    pass_gathers(1)
     give_back(0)
     row_gradients(1)
     give_back(1)
-    for h in range(2):
+    for g in range(4):
         for i in range(1, PARTS):
-            hidden_copy(h, i)[0].start()
+            hidden_copy(g, i)[0].start()
 
     stores = []
 
@@ -359,17 +377,17 @@
 
     weight_gradient(0, gate_grad, gate_grad_hbm)
     weight_gradient(1, up_grad, up_grad_hbm)
-    for h in range(2):
+    for g in range(4):
         for i in range(1, PARTS):
-            hidden_copy(h, i)[1].wait()
+            hidden_copy(g, i)[1].wait()
     hidden = hid[...].reshape(2 * experts, hidden_dim)
     down_grad[...] = matmul(hidden, grad_all[...], 0, 0).astype(BF)
     store(2, down_grad, down_grad_hbm.at[0])
 
-    for h in range(2):
+    for g in range(4):
         for i in range(6):
-            sums(h, i).wait_send()
-            gathers(h, i).wait_send()
+            sums(g, i).wait_send()
+            gathers(g, i).wait_send()
     pieces = fin.reshape(experts, units, LANES)
     for same in range(2):
         count = block - 1 if same else block
@@ -381,8 +399,7 @@
                 def _():
                     remote(part, part, r_send.at[h], r_recv, sibling).wait_send()
 
-    part = pl.ds(0, 2 * n - 1)
-    moved = recv.reshape(2 * n, n, 2 * units, LANES).at[part]
+    moved = recv.reshape(4 * n, n, units, LANES).at[pl.ds(0, 4 * n - 2)]
     remote(moved, moved, s2_send, s2_recv.at[0], sibling).wait_send()
 
     part = pieces.at[pl.ds(0, experts - 1)]
@@ -431,7 +448,7 @@
     chosen = routes.shape[1]
     _, _, hidden_dim = gate_weight.shape
     units = 2 * width // LANES
-    span = experts // PARTS
+    span = experts // (2 * PARTS)
     hbm = pl.BlockSpec(memory_space=pltpu.HBM)
     dma = pltpu.SemaphoreType.DMA
 
@@ -456,24 +473,24 @@
             buf(width, hidden_dim), buf(width, hidden_dim), buf(hidden_dim, width),
             buf(count_tok, width),
             buf(width, hidden_dim), buf(width, hidden_dim), buf(hidden_dim, width),
-            buf(n, n, 2 * units, LANES), buf(n, n, 2 * units, LANES),
-            buf(n, n, 2 * units, LANES), buf(n, n, 2 * units, LANES),
-            buf(2, n, n, 2 * units, LANES),
+            buf(2, n, n, units, LANES), buf(2, n, n, units, LANES),
+            buf(2, n, n, units, LANES), buf(2, n, n, units, LANES),
+            buf(4, n, n, units, LANES),
             buf(2 * experts, width), buf(2 * experts, width),
-            buf(2, n, n, 2 * units, LANES),
-            buf(2, PARTS, span, 3 * hidden_dim),
-            buf(2, 2, span // 2, 3 * hidden_dim),
-            buf(2, 2, span // 2, 3 * hidden_dim),
-            buf(2, 2, span, 3 * hidden_dim),
-            buf(2, PARTS, span, 2 * hidden_dim),
-            buf(2, PARTS, span, hidden_dim),
+            buf(2, 2, n, n, units, LANES),
+            buf(4, PARTS, span, 3 * hidden_dim),
+            buf(4, 2, span, 3 * hidden_dim // 2),
+            buf(4, 2, span, 3 * hidden_dim // 2),
+            buf(4, 2, span, 3 * hidden_dim),
+            buf(4, PARTS, span, 2 * hidden_dim),
+            buf(4, PARTS, span, hidden_dim),
             buf(2, n, n, units, LANES), buf(2, n, n, units, LANES),
-            buf(experts * 2 * units, LANES, dtype=F32),
+            buf(2, experts * units, LANES, dtype=F32),
             buf(experts * units, LANES, dtype=F32),
             buf(2, experts, count_tok),
-            dma((8,)), dma((4,)), pltpu.SemaphoreType.REGULAR,
-            dma((2,)), dma((2,)), dma, dma((2,)),
-            dma((2, 6)), dma((2, 6)), dma((2, 6)), dma((2, 6)), dma((2, 3)), dma((2, 3)),
+            dma((8,)), dma((4,)),
+            dma((2, 2)), dma((2, 2)), dma, dma((4,)),
+            dma((4, 6)), dma((4, 6)), dma((4, 6)), dma((4, 6)), dma((4, 3)), dma((4, 3)),
             dma((2,)), dma,
         ],
         compiler_params=pltpu.CompilerParams(

time: 64.8 us -> 62.5 us (0.965)
  Pallas kernels: 64 us -> 61.7 us
    pallas_call x1, Pallas kernels: 61.3 us -> 59 us  [local(): pl.pallas_call(functools.partial(kernel, side), out_shape=shapes, in_spec...]
where the time goes in v4:
time: 62.5 us; the launch traced here: 62.3 us
  Pallas kernels  61.7 us (99%)
  between operations  0.64 us (1%)
    pallas_call x1, Pallas kernels, local(): pl.pallas_call(functools.partial(kernel, side), out_shape=shapes, in_spec...  59 us
    pallas_call x1, Pallas kernels, local(): pl.pallas_call(hand_over, out_shape=shapes, in_specs=[hbm] * 4, out_specs...  2.71 us

profile of v4, /device:TPU:1, one launch (start us, length us, event | category | flops | bytes accessed | tf_op | source)
XLA Modules:
  0.0 62.3 jit_solution(4892559933478251025)
XLA Ops:
  0.6 59.0 %expert_backward.1 = (bf16[32,512]{1,0:T(8,128)(2,1)}, bf16[1,512,768]{2,1,0:T(8,128)(2,1)}, bf16[1,512,768]{2,1,0:T(8,128)(2,1)}, bf16[1,768,512]{2,1,0:T(8,128)(2,1)}) custom-call(bf16[32,512]{1,0:T(8,128)(2,1)} %tokens_hbm.1, bf16[32,512]{1,0:T(8,128)(2,1)} %out_grad_hbm.1, s32[8,32]{1,0:T(8,128)} %bitcast.3, f32[8,32]{1,0:T(8,128)} %bitcast.4, ...), custom_call_target="tpu_custom_call" | custom-call | tf_op jit(solution)/shard_map/expert_backward/pallas_call | solution.py:464
  59.6 2.7 %hand_over.1 = (bf16[32,512]{1,0:T(8,128)(2,1)}, bf16[1,512,768]{2,1,0:T(8,128)(2,1)}, bf16[1,512,768]{2,1,0:T(8,128)(2,1)}, bf16[1,768,512]{2,1,0:T(8,128)(2,1)}) custom-call(bf16[32,512]{1,0:T(8,128)(2,1)} %get-tuple-element.8.refs_0_, bf16[1,512,768]{2,1,0:T(8,128)(2,1)} %get-tuple-element.9.refs_1_, bf16[1,512,768]{2,1,0:T(8,128)(2,1)} %get-tuple-element.10.refs_2_, ...), custom_call_target="tpu_custom_call" | custom-call | tf_op jit(solution)/shard_map/hand_over/pallas_call | solution.py:504

commit v5 on v4

--- a/solution.py
+++ b/solution.py
@@ -180,10 +180,6 @@
     first_stage(0)
     prepare(1)
     first_stage(1)
-    for r in range(2):
-        for p in range(2):
-            first_copy(r, p).wait_send()
-
     second_stage(0)
     second_stage(1)
 
@@ -260,10 +256,12 @@
         psend[g, :, :, hidden_dim:double] = (
             matmul(rows_all[rows, :], up[...]).astype(BF).reshape(shape)
         )
+        for i in (0, 3):
+            sums(g, i).start()
         psend[g, :, :, double:] = (
             matmul(grad_all[rows, :], down[...], 1, 1).astype(BF).reshape(shape)
         )
-        for i in range(4):
+        for i in (1, 2):
             sums(g, i).start()
 
     def pass_sums(g):
@@ -293,8 +291,10 @@
         full[g, d, :, 0:hidden_dim] = (
             hidden_grad * up_sum * sigma * (1.0 + gate_sum * (1.0 - sigma))
         ).astype(BF)
+        for i in (0, 3):
+            gathers(g, i).start()
         full[g, d, :, hidden_dim:] = (hidden_grad * active).astype(BF)
-        for i in range(4):
+        for i in (1, 2):
             gathers(g, i).start()
         hid[g, d] = (active * up_sum).astype(BF)
 
@@ -399,6 +399,9 @@
                 def _():
                     remote(part, part, r_send.at[h], r_recv, sibling).wait_send()
 
+    for r in range(2):
+        for p in range(2):
+            first_copy(r, p).wait_send()
     moved = recv.reshape(4 * n, n, units, LANES).at[pl.ds(0, 4 * n - 2)]
     remote(moved, moved, s2_send, s2_recv.at[0], sibling).wait_send()
 
@@ -423,7 +426,7 @@
     pieces = []
     for i in range(count):
         rows = given[i].shape[-2]
-        step = max(rows // 4, min(rows, 32))
+        step = max(rows // 2, min(rows, 32))
         for at in range(0, rows, step):
             part = (0, pl.ds(at, step)) if len(given[i].shape) == 3 else (pl.ds(at, step),)
             pieces.append((given[i].at[part], passed[i].at[part], kept[i].at[part]))

time: 62.5 us -> 62.2 us (level)
  no operation moved by 1% of the time
where the time goes in v5:
time: 62.2 us; the launch traced here: 62 us
  Pallas kernels  61.4 us (99%)
  between operations  0.64 us (1%)
    pallas_call x1, Pallas kernels, local(): pl.pallas_call(functools.partial(kernel, side), out_shape=shapes, in_spec...  58.7 us
    pallas_call x1, Pallas kernels, local(): pl.pallas_call(hand_over, out_shape=shapes, in_specs=[hbm] * 4, out_specs...  2.69 us

profile of v5, /device:TPU:1, one launch (start us, length us, event | category | flops | bytes accessed | tf_op | source)
XLA Modules:
  0.0 62.0 jit_solution(16067042495728975361)
XLA Ops:
  0.6 58.7 %expert_backward.1 = (bf16[32,512]{1,0:T(8,128)(2,1)}, bf16[1,512,768]{2,1,0:T(8,128)(2,1)}, bf16[1,512,768]{2,1,0:T(8,128)(2,1)}, bf16[1,768,512]{2,1,0:T(8,128)(2,1)}) custom-call(bf16[32,512]{1,0:T(8,128)(2,1)} %tokens_hbm.1, bf16[32,512]{1,0:T(8,128)(2,1)} %out_grad_hbm.1, s32[8,32]{1,0:T(8,128)} %bitcast.3, f32[8,32]{1,0:T(8,128)} %bitcast.4, ...), custom_call_target="tpu_custom_call" | custom-call | tf_op jit(solution)/shard_map/expert_backward/pallas_call | solution.py:467
  59.3 2.7 %hand_over.1 = (bf16[32,512]{1,0:T(8,128)(2,1)}, bf16[1,512,768]{2,1,0:T(8,128)(2,1)}, bf16[1,512,768]{2,1,0:T(8,128)(2,1)}, bf16[1,768,512]{2,1,0:T(8,128)(2,1)}) custom-call(bf16[32,512]{1,0:T(8,128)(2,1)} %get-tuple-element.8.refs_0_, bf16[1,512,768]{2,1,0:T(8,128)(2,1)} %get-tuple-element.9.refs_1_, bf16[1,512,768]{2,1,0:T(8,128)(2,1)} %get-tuple-element.10.refs_2_, ...), custom_call_target="tpu_custom_call" | custom-call | tf_op jit(solution)/shard_map/hand_over/pallas_call | solution.py:507
